TPU v7x, 32 devices: a whole 2x2x4 slice. The times are simulated.
32 devices in a mesh: bond: 4 (over y, core), atom: 8 (over z, x).
Axes of the slice: x: 2, y: 2, z: 4, core: 2. Of those that a mesh axis runs over, the one named last changes fastest.
Arguments:
- bond_states: bfloat16 [65536, 512], P(('bond', 'atom')), may hold values from -6 to 6
- block_counts: int32 [32], P(('bond', 'atom')), may hold values from 8 to 64, as said below
- send_rows: int32 [32, 32, 64], P(('bond', 'atom')), may hold values from 0 to 2047
- source_slots: int32 [32, 2048], P(('bond', 'atom')), may hold values from 0 to 2047
- target_slots: int32 [32, 2048], P(('bond', 'atom')), may hold values from 0 to 1023
- return_rows: int32 [32, 1024], P(('bond', 'atom')), may hold values from 0 to 2047
- angular_basis: bfloat16 [2048, 32, 512], P(('bond', 'atom')), may hold values from -1 to 1
- pre_inner: bfloat16 [2, 512, 512], replicated, may hold values from -0.25 to 0.25
- pre_outer: bfloat16 [2, 512, 512], replicated, may hold values from -0.25 to 0.25
- down_proj: bfloat16 [2, 512, 64], replicated, may hold values from -0.25 to 0.25
- bilinear: bfloat16 [2, 1024, 64], replicated, may hold values from -0.1875 to 0.1875
- up_proj: bfloat16 [2, 64, 512], replicated, may hold values from -0.75 to 0.75
- post_inner: bfloat16 [2, 512, 512], replicated, may hold values from -0.25 to 0.25
- post_outer: bfloat16 [2, 512, 512], replicated, may hold values from -0.25 to 0.25
Outputs:
- bond_out: bfloat16 [65536, 512], P(('bond', 'atom'))
Inputs may be any that keep to these rules, and one draw needn't show every extreme that they name: Owner o's blocks numbered below block_counts[o] are live, the others are padding; some owner has all 64 live in every draw.
All inputs are finite; a program needn't handle non-finite values.
Results may differ from a plain program's by a relative error of at most 0.0078.
Values may be sent and summed in bfloat16 or wider, within the bound.
No kernel may reach another device: no remote copies, remote signals or barrier semaphores. Data moves between devices by JAX's collectives and lax.ppermute only.
A program may use at most 128 MiB of HBM per device.

v0:
```python
import functools

import jax
import jax.numpy as jnp
from jax import lax
from jax.experimental import pallas as pl
from jax.experimental.pallas import tpu as pltpu
from jax.sharding import PartitionSpec as P

root_half = 0.7071067811865476
LANES = 128
HIGH = 256
BLOCKS_IN_GROUP = 8
SLOT_ROWS = 8
VMEM_BYTES = 48 * 1024 * 1024

bf16 = jnp.bfloat16
f32 = jnp.float32
i32 = jnp.int32


def mm(a, b):
    return jnp.dot(a, b, preferred_element_type=f32)


def mm_nt(a, b):
    return lax.dot_general(a, b, (((1,), (1,)), ((), ())), preferred_element_type=f32)


def silu_of_half(u):
    return u + u * jnp.tanh(u)


def half_weight(ref):
    return ref[...] * bf16(0.5)


def lane(shape):
    return lax.broadcasted_iota(i32, shape, 1)


def one_hot_rows(high):
    at = lane(high.shape)
    parts = [jnp.where(high == at + k * LANES, f32(1), f32(0)).astype(bf16) for k in range(HIGH // LANES)]
    return jnp.concatenate(parts, axis=1)


def column(row):
    return jnp.transpose(jnp.broadcast_to(row, (LANES, LANES)))


def swap_halves(v):
    return pltpu.roll(v, v.shape[1] // 2, 1)


def pick_group(wide, group, count):
    picked = wide[:, :LANES]
    for m in range(1, count):
        picked = jnp.where(group == m, wide[:, m * LANES : (m + 1) * LANES], picked)
    return picked


def residual_rows(x, inner_half, outer_half):
    hidden = silu_of_half(mm(x, inner_half)).astype(bf16)
    return ((x.astype(f32) + silu_of_half(mm(hidden, outer_half))) * root_half).astype(bf16)


def project_pair(inner_rows, down_t):
    zero = jnp.zeros_like(down_t)
    left = jnp.concatenate([down_t, zero], axis=0)
    right = jnp.concatenate([zero, down_t], axis=0)
    u = mm_nt(inner_rows[:HIGH], left) + mm_nt(inner_rows[HIGH:], right)
    return silu_of_half(u).astype(bf16)


def write_payload(send_ref, table_ref, payload_ref):
    owners, cap = send_ref.shape
    half_cap = cap // 2
    pack = LANES // half_cap
    groups = table_ref.shape[1] // LANES
    table = table_ref[...]
    low_half = lane((LANES, LANES)) < LANES // 2
    for first in range(0, owners, pack):
        columns = [
            jnp.transpose(jnp.concatenate([jnp.broadcast_to(send_ref[o : o + 1, :], (LANES, cap))] * (LANES // cap), axis=1))
            for o in range(first, first + pack)
        ]
        sides = []
        for side in range(2):
            rows = jnp.concatenate([c[side * half_cap : (side + 1) * half_cap] for c in columns], axis=0)
            wide = mm(one_hot_rows(rows & (HIGH - 1)), table)
            low = rows >> 8
            picked = pick_group(wide, low >> 1, groups)
            sides.append(jnp.where((low & 1) == side, picked, swap_halves(picked)))
        packed = jnp.where(low_half, sides[0], sides[1]).astype(bf16)
        payload_ref[first * half_cap : (first + pack) * half_cap, :] = packed


def first_kernel(x_ref, send_ref, inner_ref, outer_ref, down_ref, out_ref, payload_ref, table_ref):
    step = pl.program_id(0)
    rows = residual_rows(x_ref[...], half_weight(inner_ref), half_weight(outer_ref))
    out_ref[...] = rows
    table_ref[:, pl.ds(pl.multiple_of(step * LANES, LANES), LANES)] = project_pair(rows, half_weight(down_ref))

    @pl.when(step == pl.num_programs(0) - 1)
    def _():
        write_payload(send_ref, table_ref, payload_ref)


def gather_messages(incoming_ref, return_pick_ref, return_low_ref, message_ref):
    slots = incoming_ref.shape[0]
    low_half = lane((slots, LANES)) < LANES // 2
    upper = jnp.where(low_half, 0, 1)
    groups = message_ref.shape[1] // LANES
    pieces = []
    for g in range(return_low_ref.shape[0]):
        m, side = divmod(g, 2)
        both = incoming_ref[:, m * LANES : (m + 1) * LANES].astype(f32)
        other = swap_halves(both)
        spread = jnp.where(low_half, both, other) if side == 0 else jnp.where(low_half, other, both)
        low = return_low_ref[g]
        pieces.append(
            jnp.concatenate(
                [jnp.where(low == 2 * k + upper, spread, f32(0)).astype(bf16) for k in range(groups)], axis=1
            )
        )
    message_ref[...] = mm(return_pick_ref[...], jnp.concatenate(pieces, axis=0)).astype(bf16)


def join_rows(inner, message, up_half):
    zero = jnp.zeros_like(up_half)
    u = jnp.concatenate(
        [
            mm(message, jnp.concatenate([up_half, zero], axis=0)),
            mm(message, jnp.concatenate([zero, up_half], axis=0)),
        ],
        axis=0,
    )
    return ((inner.astype(f32) + silu_of_half(u)) * root_half).astype(bf16)


def middle_kernel(
    incoming_ref,
    return_pick_ref,
    return_low_ref,
    x_ref,
    up_ref,
    post_inner_ref,
    post_outer_ref,
    send_ref,
    inner_ref,
    outer_ref,
    down_ref,
    out_ref,
    payload_ref,
    message_ref,
    table_ref,
):
    step = pl.program_id(0)

    @pl.when(step == 0)
    def _():
        gather_messages(incoming_ref, return_pick_ref, return_low_ref, message_ref)

    at = pl.ds(pl.multiple_of(step * LANES, LANES), LANES)
    joined = join_rows(x_ref[...], message_ref[:, at], half_weight(up_ref))
    state = residual_rows(joined, half_weight(post_inner_ref), half_weight(post_outer_ref))
    rows = residual_rows(state, half_weight(inner_ref), half_weight(outer_ref))
    out_ref[...] = rows
    table_ref[:, at] = project_pair(rows, half_weight(down_ref))

    @pl.when(step == pl.num_programs(0) - 1)
    def _():
        write_payload(send_ref, table_ref, payload_ref)


def last_kernel(
    incoming_ref, return_pick_ref, return_low_ref, x_ref, up_ref, post_inner_ref, post_outer_ref, out_ref, message_ref
):
    step = pl.program_id(0)

    @pl.when(step == 0)
    def _():
        gather_messages(incoming_ref, return_pick_ref, return_low_ref, message_ref)

    at = pl.ds(pl.multiple_of(step * LANES, LANES), LANES)
    joined = join_rows(x_ref[...], message_ref[:, at], half_weight(up_ref))
    out_ref[...] = residual_rows(joined, half_weight(post_inner_ref), half_weight(post_outer_ref))


def prepare_kernel(
    cap,
    cap_back,
    counts_ref,
    source_ref,
    target_ref,
    return_ref,
    basis_ref,
    bilinear_ref,
    basis_out,
    weight_out,
    source_pick_out,
    source_code_out,
    target_pick_out,
    target_low_out,
    return_pick_out,
    return_low_out,
):
    blocks, width, span = basis_ref.shape
    sph = span // width
    layers, trip, _ = bilinear_ref.shape
    groups = blocks // BLOCKS_IN_GROUP
    chunks = source_ref.shape[1] // LANES
    side_blocks = LANES // width
    half_cap = cap // 2
    to = lax.broadcasted_iota(i32, (span, span), 0)
    order = jnp.where(lane((span, span)) == (to % width) * sph + to // width, f32(1), f32(0)).astype(bf16)
    for g in range(groups):
        rows = jnp.concatenate(
            [
                basis_ref[g * side_blocks : (g + 1) * side_blocks].reshape(LANES, span),
                basis_ref[blocks // 2 + g * side_blocks : blocks // 2 + (g + 1) * side_blocks].reshape(LANES, span),
            ],
            axis=0,
        )
        basis_out[g] = mm_nt(order, rows).astype(bf16)
    zero = jnp.zeros((trip, LANES), bf16)
    for layer in range(layers):
        for k in range(0, sph, 2):
            pair = jnp.transpose(bilinear_ref[layer, :, k * trip : (k + 2) * trip].astype(f32))
            both = jnp.concatenate([pair, pair], axis=1).astype(bf16)
            for j in range(2):
                w = both[j * trip : (j + 1) * trip]
                base = (k + j) * 2 * trip
                weight_out[layer, base : base + trip, :] = jnp.concatenate([w, zero], axis=1)
                weight_out[layer, base + trip : base + 2 * trip, :] = jnp.concatenate([zero, w], axis=1)
    for chunk in range(chunks):
        side, g = divmod(chunk, groups)
        s = column(source_ref[:, chunk * LANES : (chunk + 1) * LANES])
        rho = (s // cap) * half_cap + s % half_cap
        half = (s // half_cap) % 2
        rows = slice(side * LANES, (side + 1) * LANES)
        source_pick_out[g, rows, :] = one_hot_rows(rho & (HIGH - 1))
        source_code_out[g, rows, :] = (rho >> 8) * 2 + (half ^ side)
    count = counts_ref[0]
    highs = target_pick_out.shape[0]
    for chunk in range(chunks):
        cols = slice(chunk * LANES, (chunk + 1) * LANES)
        row = target_ref[:, cols]
        target_low_out[cols, :] = (column(row) % cap_back) // SLOT_ROWS
        high = (row // cap_back) * SLOT_ROWS + row % SLOT_ROWS
        live = (lane(row.shape) + chunk * LANES) // width < count
        high = jnp.broadcast_to(jnp.where(live, high, -1), (LANES, LANES))
        for h in range(highs // LANES):
            at = lax.broadcasted_iota(i32, (LANES, LANES), 0) + h * LANES
            target_pick_out[h * LANES : (h + 1) * LANES, cols] = jnp.where(high == at, f32(1), f32(0)).astype(bf16)
    parts = cap_back // SLOT_ROWS
    owners_in = LANES // cap_back
    for chunk in range(return_ref.shape[1] // LANES):
        col = column(return_ref[:, chunk * LANES : (chunk + 1) * LANES])
        for o in range(owners_in):
            for g in range(parts):
                base = (chunk * owners_in + o) * SLOT_ROWS
                return_low_out[g, base : base + SLOT_ROWS, :] = col[(o * parts + g) * SLOT_ROWS : (o * parts + g + 1) * SLOT_ROWS]
    slots = return_low_out.shape[1]
    for g in range(parts):
        for chunk in range(slots // LANES):
            rows = slice(chunk * LANES, (chunk + 1) * LANES)
            r = return_low_out[g, rows, :]
            high = jnp.transpose(r) & (HIGH - 1)
            return_low_out[g, rows, :] = r >> 8
            for h in range(HIGH // LANES):
                at = lax.broadcasted_iota(i32, (LANES, LANES), 0) + h * LANES
                cols = slice(g * slots + chunk * LANES, g * slots + (chunk + 1) * LANES)
                return_pick_out[h * LANES : (h + 1) * LANES, cols] = jnp.where(high == at, f32(1), f32(0)).astype(bf16)


def owner_kernel(
    arrived_ref,
    source_pick_ref,
    source_code_ref,
    basis_ref,
    weight_ref,
    target_low_ref,
    target_pick_ref,
    out_ref,
    spread_ref,
):
    step = pl.program_id(0)
    span = basis_ref.shape[0]
    width = LANES // (BLOCKS_IN_GROUP // 2)
    sph = span // width
    tables = arrived_ref.shape[0] // HIGH
    table = jnp.concatenate([arrived_ref[m * HIGH : (m + 1) * HIGH, :] for m in range(tables)], axis=1)
    wide = mm(source_pick_ref[...], table)
    code = source_code_ref[...]
    picked = pick_group(wide, code >> 1, tables)
    turned = jnp.where((code & 1) == 1, swap_halves(picked), picked)
    row = lax.broadcasted_iota(i32, turned.shape, 0)
    upper_lane = lane(turned.shape) >= LANES // 2
    kept = jnp.where((row >= LANES) == upper_lane, turned, f32(0)).astype(bf16)
    columns = []
    for j in range(BLOCKS_IN_GROUP // 2):
        pieces = []
        for side in range(2):
            for k in range(BLOCKS_IN_GROUP // 2):
                base = side * LANES + k * width
                pieces.append(kept[base : base + width] if k == j else jnp.zeros((width, LANES), bf16))
        columns.append(jnp.concatenate(pieces, axis=0))
    contracted = mm(basis_ref[...], jnp.concatenate(columns, axis=1)).astype(bf16)
    lhs = jnp.concatenate(
        [
            jnp.concatenate(
                [contracted[k * width : (k + 1) * width, j * LANES : (j + 1) * LANES] for k in range(sph)], axis=1
            )
            for j in range(BLOCKS_IN_GROUP // 2)
        ],
        axis=0,
    )
    partial = mm(lhs, weight_ref[...])
    upper = jnp.where(lane((LANES, LANES)) < LANES // 2, 0, 1)
    groups = spread_ref.shape[1] // LANES
    half_rows = spread_ref.shape[0] // 2
    for side in range(2):
        rows = pl.ds(pl.multiple_of(side * half_rows + step * LANES, LANES), LANES)
        low = target_low_ref[rows, :]
        values = partial[:, side * LANES : (side + 1) * LANES]
        for m in range(groups):
            spread_ref[rows, m * LANES : (m + 1) * LANES] = jnp.where(low == 2 * m + upper, values, f32(0)).astype(bf16)

    @pl.when(step == pl.num_programs(0) - 1)
    def _():
        out_ref[...] = mm(target_pick_ref[...], spread_ref[...]).astype(bf16)


def whole(shape):
    return pl.BlockSpec(shape, lambda *_: (0,) * len(shape))


def of_layer(shape, layer):
    return pl.BlockSpec((None,) + shape[1:], lambda *_: (layer,) + (0,) * (len(shape) - 1))


def params():
    return pltpu.CompilerParams(vmem_limit_bytes=VMEM_BYTES, dimension_semantics=("arbitrary",))


def on_device(
    bond_states,
    block_counts,
    send_rows,
    source_slots,
    target_slots,
    return_rows,
    angular_basis,
    pre_inner,
    pre_outer,
    down_proj,
    bilinear,
    up_proj,
    post_inner,
    post_outer,
):
    axes = ("bond", "atom")
    peers = lax.axis_size("bond") * lax.axis_size("atom")
    rows, depth = bond_states.shape
    blocks, width, span = angular_basis.shape
    layers, _, trip = down_proj.shape
    cap = send_rows.shape[2]
    returns = return_rows.shape[1]
    cap_back = returns // peers
    pair = 2 * HIGH
    steps = rows // pair
    lookup = peers * cap // 2
    slots = peers * SLOT_ROWS
    slot_lanes = cap_back // SLOT_ROWS * trip
    groups = blocks // BLOCKS_IN_GROUP
    group_rows = BLOCKS_IN_GROUP * width
    send = send_rows.reshape(peers, cap)
    down_t = jnp.swapaxes(down_proj, 1, 2)
    bilinear_t = jnp.swapaxes(bilinear, 1, 2)
    row_block = pl.BlockSpec((pair, depth), lambda i: (i, 0))
    row_shape = jax.ShapeDtypeStruct((rows, depth), bf16)
    payload_shape = jax.ShapeDtypeStruct((lookup, LANES), bf16)
    table_scratch = pltpu.VMEM((HIGH, rows // HIGH * trip), bf16)

    def exchange(values, per_peer):
        values = values.reshape(peers, per_peer, values.shape[1])
        got = lax.all_to_all(values, axes, split_axis=0, concat_axis=0, tiled=True)
        return got.reshape(peers * per_peer, values.shape[2])

    inner, payload = pl.pallas_call(
        first_kernel,
        grid=(steps,),
        in_specs=[
            row_block,
            whole(send.shape),
            of_layer(pre_inner.shape, 0),
            of_layer(pre_outer.shape, 0),
            of_layer(down_t.shape, 0),
        ],
        out_specs=[row_block, whole(payload_shape.shape)],
        out_shape=[row_shape, payload_shape],
        scratch_shapes=[table_scratch],
        compiler_params=params(),
        name="first",
    )(bond_states, send, pre_inner, pre_outer, down_t)

    prepared_shapes = [
        jax.ShapeDtypeStruct((groups, span, group_rows), bf16),
        jax.ShapeDtypeStruct((layers, bilinear.shape[1] * 2, 2 * LANES), bf16),
        jax.ShapeDtypeStruct((groups, group_rows, HIGH), bf16),
        jax.ShapeDtypeStruct((groups, group_rows, LANES), i32),
        jax.ShapeDtypeStruct((slots, blocks * width), bf16),
        jax.ShapeDtypeStruct((blocks * width, LANES), i32),
        jax.ShapeDtypeStruct((HIGH, returns), bf16),
        jax.ShapeDtypeStruct((cap_back // SLOT_ROWS, slots, LANES), i32),
    ]
    prepared = pl.pallas_call(
        functools.partial(prepare_kernel, cap, cap_back),
        in_specs=[pl.BlockSpec(memory_space=pltpu.SMEM)] + [pl.BlockSpec(memory_space=pltpu.VMEM)] * 5,
        out_specs=[pl.BlockSpec(memory_space=pltpu.VMEM)] * len(prepared_shapes),
        out_shape=prepared_shapes,
        compiler_params=pltpu.CompilerParams(vmem_limit_bytes=VMEM_BYTES),
        cost_estimate=pl.CostEstimate(flops=4 * 10**9, bytes_accessed=12 * 10**6, transcendentals=0),
        name="prepare",
    )(block_counts, source_slots, target_slots, return_rows, angular_basis, bilinear_t)
    basis, weight, source_pick, source_code, target_pick, target_low, return_pick, return_low = prepared

    out = None
    for layer in range(layers):
        arrived = exchange(payload, cap // 2)
        slot_sums = pl.pallas_call(
            owner_kernel,
            grid=(groups,),
            in_specs=[
                whole(arrived.shape),
                pl.BlockSpec((None, group_rows, HIGH), lambda i: (i, 0, 0)),
                pl.BlockSpec((None, group_rows, LANES), lambda i: (i, 0, 0)),
                pl.BlockSpec((None, span, group_rows), lambda i: (i, 0, 0)),
                of_layer(weight.shape, layer),
                whole(target_low.shape),
                whole(target_pick.shape),
            ],
            out_specs=whole((slots, slot_lanes)),
            out_shape=jax.ShapeDtypeStruct((slots, slot_lanes), bf16),
            scratch_shapes=[pltpu.VMEM((blocks * width, slot_lanes), bf16)],
            compiler_params=params(),
            name="owner",
        )(arrived, source_pick, source_code, basis, weight, target_low, target_pick)
        incoming = exchange(slot_sums, SLOT_ROWS)
        head = [incoming, return_pick, return_low, inner, up_proj, post_inner, post_outer]
        head_specs = [
            whole(incoming.shape),
            whole(return_pick.shape),
            whole(return_low.shape),
            row_block,
            of_layer(up_proj.shape, layer),
            of_layer(post_inner.shape, layer),
            of_layer(post_outer.shape, layer),
        ]
        message_scratch = pltpu.VMEM((HIGH, rows // HIGH * trip), bf16)
        if layer + 1 < layers:
            inner, payload = pl.pallas_call(
                middle_kernel,
                grid=(steps,),
                in_specs=head_specs
                + [
                    whole(send.shape),
                    of_layer(pre_inner.shape, layer + 1),
                    of_layer(pre_outer.shape, layer + 1),
                    of_layer(down_t.shape, layer + 1),
                ],
                out_specs=[row_block, whole(payload_shape.shape)],
                out_shape=[row_shape, payload_shape],
                scratch_shapes=[message_scratch, table_scratch],
                compiler_params=params(),
                name="middle",
            )(*head, send, pre_inner, pre_outer, down_t)
        else:
            out = pl.pallas_call(
                last_kernel,
                grid=(steps,),
                in_specs=head_specs,
                out_specs=row_block,
                out_shape=row_shape,
                scratch_shapes=[message_scratch],
                compiler_params=params(),
                name="last",
            )(*head)
    return out


def solution(mesh):
    split = ("bond", "atom")
    in_specs = (
        P(split, None),
        P(split),
        P(split, None, None),
        P(split, None),
        P(split, None),
        P(split, None),
        P(split, None, None),
    ) + (P(),) * 7
    return jax.shard_map(on_device, mesh=mesh, in_specs=in_specs, out_specs=P(split, None), check_vma=False)
```

profile of v0, /device:TPU:0, one launch (start us, length us, event | category | flops | bytes accessed | tf_op | source)
XLA Modules:
  0.0 107.6 jit_solution(11840126846489083154)
XLA Ops:
  0.0 0.0 copy-start.3
  0.0 1.2 %copy-done.3 = bf16[2,512,512]{2,1,0:T(8,128)(2,1)S(1)} copy-done((bf16[2,512,512]{2,1,0:T(8,128)(2,1)S(1)}, bf16[2,512,512]{2,1,0:T(8,128)(2,1)}, u32[]{:S(2)}) %copy-start.3) | copy-done | bytes 1048600
  1.2 0.0 copy-start.5
  1.2 1.2 %copy-done.5 = bf16[2,512,512]{2,1,0:T(8,128)(2,1)S(1)} copy-done((bf16[2,512,512]{2,1,0:T(8,128)(2,1)S(1)}, bf16[2,512,512]{2,1,0:T(8,128)(2,1)}, u32[]{:S(2)}) %copy-start.5) | copy-done | bytes 1048600
  2.5 0.0 copy-start.15
  2.5 0.9 copy-done.15
  3.4 0.0 copy-start.18
  3.4 0.7 copy-done.18
  4.1 0.0 copy-start.21
  4.1 0.0 copy-start.22
  4.1 0.0 copy-start.23
  4.1 8.9 %first.1 = (bf16[2048,512]{1,0:T(8,128)(2,1)S(1)}, bf16[1024,128]{1,0:T(8,128)(2,1)}) custom-call(bf16[2048,512]{1,0:T(8,128)(2,1)} %x_ref.1, s32[32,64]{1,0:T(8,128)S(1)} %bitcast.20, bf16[2,512,512]{2,1,0:T(8,128)(2,1)S(1)} %copy-done.3, bf16[2,512,512]{2,1,0:T(8,128)(2,1)S(1)} %copy-done.5, bf16[2,64,512]{2,1,0:T(8,128)(2,1)S(1)} %bitcast.13), custom_call_target="tpu_custom_call" | custom-call | tf_op jit(solution)/shard_map/first/pallas_call | solution.py:392
  13.0 0.0 copy-start.9
  13.0 1.3 %copy-done.9 = bf16[2048,512]{1,0:T(8,128)(2,1)} copy-done((bf16[2048,512]{1,0:T(8,128)(2,1)}, bf16[2048,512]{1,0:T(8,128)(2,1)S(1)}, u32[]{:S(2)}) %copy-start.9) | copy-done | bytes 2097176
  14.3 7.3 %all-to-all-start = ((bf16[32,32,128]{2,1,0:T(8,128)(2,1)}), bf16[32,32,128]{2,1,0:T(8,128)(2,1)S(1)}, u32[]{:S(2)}, u32[]{:S(2)}) async-start(bf16[32,32,128]{2,1,0:T(8,128)(2,1)} %bitcast.2), calls=%async_computation | async-start | bytes 524288 | tf_op jit(solution)/shard_map/all_to_all | solution.py:389
  22.3 0.0 copy-done.21
  22.3 0.0 copy-done.22
  22.3 0.0 copy-done.23
  22.3 0.0 copy-start.20
  22.3 0.9 copy-done.20
  23.2 7.2 %prepare.1 = (bf16[8,512,256]{2,1,0:T(8,128)(2,1)}, bf16[2,2048,256]{2,1,0:T(8,128)(2,1)}, bf16[8,256,256]{2,1,0:T(8,128)(2,1)S(1)}, s32[8,256,128]{2,1,0:T(8,12...) custom-call(s32[1]{0:T(128)S(6)} %copy.15.counts_ref, ...), custom_call_target="tpu_custom_call" | custom-call | flops 4000000000 | bytes 12000000 | tf_op jit(solution)/shard_map/prepare/pallas_call | solution.py:419
  30.4 0.0 copy-start
  30.4 1.0 copy-done
  31.4 0.0 copy-start.11
  31.4 0.8 copy-done.11
  32.2 0.0 copy-start.13
  32.2 0.8 copy-done.13
  33.0 0.0 all-to-all-done
  33.0 0.0 copy-start.1
  33.0 1.2 %copy-done.1 = s32[2048,128]{1,0:T(8,128)S(1)} copy-done((s32[2048,128]{1,0:T(8,128)S(1)}, s32[2048,128]{1,0:T(8,128)}, u32[]{:S(2)}) %copy-start.1) | copy-done | bytes 1048600
  34.2 0.0 copy-start.4
  34.2 0.0 copy-start.6
  34.3 0.0 copy-start.7
  34.3 0.0 copy-start.8
  34.3 0.0 copy-start.12
  34.3 0.0 copy-start.14
  34.3 0.0 copy-start.16
  34.3 0.0 copy-start.17
  34.3 0.0 copy-start.19
  34.3 9.5 %owner.2 = bf16[256,256]{1,0:T(8,128)(2,1)S(1)} custom-call(bf16[1024,128]{1,0:T(8,128)(2,1)S(1)} %bitcast.11, bf16[8,256,256]{2,1,0:T(8,128)(2,1)S(1)} %get-tuple-element.18.source_pick_ref, s32[8,256,128]{2,1,0:T(8,128)S(1)} %get-tuple-element.19.source_code_ref, bf16[8,512,256]{2,1,0:T(8,128)(2,1)} %get-tuple-element.20.basis_ref, ...), custom_call_target="tpu_custom_call" | custom-call | tf_op jit(solution)/shard_map/owner/pallas_call | solution.py:433
  43.8 13.4 %all_to_all.20 = bf16[32,8,256]{2,1,0:T(8,128)(2,1)S(1)} all-to-all(bf16[32,8,256]{2,1,0:T(8,128)(2,1)S(1)} %bitcast.17), channel_id=1, replica_groups=mesh['bond'=4,'atom'=8] {'bond','atom'}, dimensions={0} | all-to-all | bytes 262144 | tf_op jit(solution)/shard_map/all_to_all | solution.py:389
  57.2 0.0 copy-done.4
  57.2 0.0 copy-done.6
  57.2 0.0 copy-done.7
  57.2 0.0 copy-done.8
  57.2 0.0 copy-done.12
  57.2 0.0 copy-done.14
  57.2 0.0 copy-done.16
  57.2 0.0 copy-done.17
  57.2 0.0 copy-done.19
  57.2 0.0 copy-start.2
  57.2 12.8 %middle.1 = (bf16[2048,512]{1,0:T(8,128)(2,1)}, bf16[1024,128]{1,0:T(8,128)(2,1)S(1)}) custom-call(bf16[256,256]{1,0:T(8,128)(2,1)S(1)} %bitcast.16, bf16[256,1024]{1,0:T(8,128)(2,1)S(1)} %copy-done.12, s32[4,256,128]{2,1,0:T(8,128)S(1)} %copy-done.14, bf16[2048,512]{1,0:T(8,128)(2,1)} %copy-done.9, bf16[2,64,512]{2,1,0:T(8,128)(2,1)S(1)} %copy-done.17, ...), custom_call_target="tpu_custom_call" | custom-call | tf_op jit(solution)/shard_map/middle/pallas_call | solution.py:464
  70.0 12.9 %all_to_all.21 = bf16[32,32,128]{2,1,0:T(8,128)(2,1)S(1)} all-to-all(bf16[32,32,128]{2,1,0:T(8,128)(2,1)S(1)} %bitcast.19), channel_id=1, replica_groups=mesh['bond'=4,'atom'=8] {'bond','atom'}, dimensions={0} | all-to-all | bytes 524288 | tf_op jit(solution)/shard_map/all_to_all | solution.py:389
  82.9 0.0 copy-done.2
  82.9 0.0 copy-start.10
  82.9 9.4 %owner.3 = bf16[256,256]{1,0:T(8,128)(2,1)S(1)} custom-call(bf16[1024,128]{1,0:T(8,128)(2,1)S(1)} %bitcast.12, bf16[8,256,256]{2,1,0:T(8,128)(2,1)S(1)} %get-tuple-element.18.source_pick_ref, s32[8,256,128]{2,1,0:T(8,128)S(1)} %get-tuple-element.19.source_code_ref, bf16[8,512,256]{2,1,0:T(8,128)(2,1)} %get-tuple-element.20.basis_ref, ...), custom_call_target="tpu_custom_call" | custom-call | tf_op jit(solution)/shard_map/owner/pallas_call | solution.py:433
  92.4 9.9 %all_to_all.22 = bf16[32,8,256]{2,1,0:T(8,128)(2,1)S(1)} all-to-all(bf16[32,8,256]{2,1,0:T(8,128)(2,1)S(1)} %bitcast.15), channel_id=1, replica_groups=mesh['bond'=4,'atom'=8] {'bond','atom'}, dimensions={0} | all-to-all | bytes 262144 | tf_op jit(solution)/shard_map/all_to_all | solution.py:389
  102.3 0.0 copy-done.10
  102.3 5.4 %last.1 = bf16[2048,512]{1,0:T(8,128)(2,1)} custom-call(bf16[256,256]{1,0:T(8,128)(2,1)S(1)} %bitcast.18, bf16[256,1024]{1,0:T(8,128)(2,1)S(1)} %copy-done.12, s32[4,256,128]{2,1,0:T(8,128)S(1)} %copy-done.14, bf16[2048,512]{1,0:T(8,128)(2,1)S(1)} %copy-done.10, bf16[2,64,512]{2,1,0:T(8,128)(2,1)S(1)} %copy-done.17, bf16[2,512,512]{2,1,0:T(8,128)(2,1)S(1)} %copy-done.7, ...), custom_call_target="tpu_custom_call" | custom-call | tf_op jit(solution)/shard_map/last/pallas_call | solution.py:481
Async XLA Ops:
  0.0 1.2 %copy-start.3 = (bf16[2,512,512]{2,1,0:T(8,128)(2,1)S(1)}, bf16[2,512,512]{2,1,0:T(8,128)(2,1)}, u32[]{:S(2)}) copy-start(bf16[2,512,512]{2,1,0:T(8,128)(2,1)} %inner_ref.3) | copy-start | bytes 3145732
  1.2 1.2 %copy-start.5 = (bf16[2,512,512]{2,1,0:T(8,128)(2,1)S(1)}, bf16[2,512,512]{2,1,0:T(8,128)(2,1)}, u32[]{:S(2)}) copy-start(bf16[2,512,512]{2,1,0:T(8,128)(2,1)} %outer_ref.3) | copy-start | bytes 3145732
  2.5 0.9 copy-start.15
  3.4 0.7 copy-start.18
  4.1 18.2 %copy-start.21 = (s32[1,2048]{1,0:T(1,128)S(1)}, s32[1,2048]{1,0:T(1,128)}, u32[]{:S(2)}) copy-start(s32[1,2048]{1,0:T(1,128)} %source_ref.1) | copy-start | bytes 24580
  4.1 18.2 %copy-start.22 = (s32[1,2048]{1,0:T(1,128)S(1)}, s32[1,2048]{1,0:T(1,128)}, u32[]{:S(2)}) copy-start(s32[1,2048]{1,0:T(1,128)} %target_ref.1) | copy-start | bytes 24580
  4.1 18.2 %copy-start.23 = (s32[1,1024]{1,0:T(1,128)S(1)}, s32[1,1024]{1,0:T(1,128)}, u32[]{:S(2)}) copy-start(s32[1,1024]{1,0:T(1,128)} %return_ref.1) | copy-start | bytes 12292
  13.0 1.3 %copy-start.9 = (bf16[2048,512]{1,0:T(8,128)(2,1)}, bf16[2048,512]{1,0:T(8,128)(2,1)S(1)}, u32[]{:S(2)}) copy-start(bf16[2048,512]{1,0:T(8,128)(2,1)S(1)} %get-tuple-element.26.x_ref) | copy-start | bytes 6291460
  14.3 18.7 %all-to-all-start = ((bf16[32,32,128]{2,1,0:T(8,128)(2,1)}), bf16[32,32,128]{2,1,0:T(8,128)(2,1)S(1)}, u32[]{:S(2)}, u32[]{:S(2)}) async-start(bf16[32,32,128]{2,1,0:T(8,128)(2,1)} %bitcast.2), calls=%async_computation | async-start | bytes 524288 | tf_op jit(solution)/shard_map/all_to_all | solution.py:389
  22.3 1.0 copy-start.20
  30.4 1.0 copy-start
  31.4 0.8 copy-start.11
  32.2 0.8 copy-start.13
  33.0 1.2 %copy-start.1 = (s32[2048,128]{1,0:T(8,128)S(1)}, s32[2048,128]{1,0:T(8,128)}, u32[]{:S(2)}) copy-start(s32[2048,128]{1,0:T(8,128)} %copy-done) | copy-start | bytes 3145732
  34.2 22.9 %copy-start.4 = (bf16[2,512,512]{2,1,0:T(8,128)(2,1)S(1)}, bf16[2,512,512]{2,1,0:T(8,128)(2,1)}, u32[]{:S(2)}) copy-start(bf16[2,512,512]{2,1,0:T(8,128)(2,1)} %inner_ref.3) | copy-start | bytes 3145732
  34.2 22.9 %copy-start.6 = (bf16[2,512,512]{2,1,0:T(8,128)(2,1)S(1)}, bf16[2,512,512]{2,1,0:T(8,128)(2,1)}, u32[]{:S(2)}) copy-start(bf16[2,512,512]{2,1,0:T(8,128)(2,1)} %outer_ref.3) | copy-start | bytes 3145732
  34.3 22.9 %copy-start.7 = (bf16[2,512,512]{2,1,0:T(8,128)(2,1)S(1)}, bf16[2,512,512]{2,1,0:T(8,128)(2,1)}, u32[]{:S(2)}) copy-start(bf16[2,512,512]{2,1,0:T(8,128)(2,1)} %post_inner_ref.3) | copy-start | bytes 3145732
  34.3 22.9 %copy-start.8 = (bf16[2,512,512]{2,1,0:T(8,128)(2,1)S(1)}, bf16[2,512,512]{2,1,0:T(8,128)(2,1)}, u32[]{:S(2)}) copy-start(bf16[2,512,512]{2,1,0:T(8,128)(2,1)} %post_outer_ref.3) | copy-start | bytes 3145732
  34.3 22.9 %copy-start.12 = (bf16[256,1024]{1,0:T(8,128)(2,1)S(1)}, bf16[256,1024]{1,0:T(8,128)(2,1)}, u32[]{:S(2)}) copy-start(bf16[256,1024]{1,0:T(8,128)(2,1)} %copy-done.11) | copy-start | bytes 1572868
  34.3 22.9 %copy-start.14 = (s32[4,256,128]{2,1,0:T(8,128)S(1)}, s32[4,256,128]{2,1,0:T(8,128)}, u32[]{:S(2)}) copy-start(s32[4,256,128]{2,1,0:T(8,128)} %copy-done.13) | copy-start | bytes 1572868
  34.3 22.9 %copy-start.16 = (bf16[2,512,64]{1,2,0:T(8,128)(2,1)S(1)}, bf16[2,512,64]{1,2,0:T(8,128)(2,1)}, u32[]{:S(2)}) copy-start(bf16[2,512,64]{1,2,0:T(8,128)(2,1)} %param.23) | copy-start | bytes 393220
  34.3 22.9 %copy-start.17 = (bf16[2,64,512]{2,1,0:T(8,128)(2,1)S(1)}, bf16[2,64,512]{2,1,0:T(8,128)(2,1)}, u32[]{:S(2)}) copy-start(bf16[2,64,512]{2,1,0:T(8,128)(2,1)} %up_ref.3) | copy-start | bytes 393220
  34.3 22.9 %copy-start.19 = (s32[1,32,64]{2,1,0:T(8,128)S(1)}, s32[1,32,64]{2,1,0:T(8,128)}, u32[]{:S(2)}) copy-start(s32[1,32,64]{2,1,0:T(8,128)} %param.16) | copy-start | bytes 24580
  57.2 25.7 %copy-start.2 = (s32[2048,128]{1,0:T(8,128)S(1)}, s32[2048,128]{1,0:T(8,128)}, u32[]{:S(2)}) copy-start(s32[2048,128]{1,0:T(8,128)} %copy-done) | copy-start | bytes 3145732
  82.9 19.4 %copy-start.10 = (bf16[2048,512]{1,0:T(8,128)(2,1)S(1)}, bf16[2048,512]{1,0:T(8,128)(2,1)}, u32[]{:S(2)}) copy-start(bf16[2048,512]{1,0:T(8,128)(2,1)} %get-tuple-element.28.x_ref) | copy-start | bytes 6291460
where the time goes:
time: 108 us
  Pallas kernels  53.1 us (49%)
  blocking collectives  36.2 us (34%)
  local copies, waits for them, and re-layouts  10.2 us (9%)
  starting transfers between devices  7.31 us (7%)
    all_to_all x3, blocking collectives, exchange(): got = lax.all_to_all(values, axes, split_axis=0, concat_axis=0, tiled=True)  36.2 us
    pallas_call x2, Pallas kernels, on_device(): pl.pallas_call(owner_kernel, grid=(groups,), in_specs=[whole(arrived.shap...  18.9 us
    pallas_call x1, Pallas kernels, on_device(): pl.pallas_call(middle_kernel, grid=(steps,), in_specs=head_specs + [whole...  12.8 us
    unnamed x48, local copies, waits for them, and re-layouts  10.2 us
    pallas_call x1, Pallas kernels, on_device(): pl.pallas_call(first_kernel, grid=(steps,), in_specs=[row_block, whole(se...  8.91 us
    all_to_all x1, starting transfers between devices, exchange(): got = lax.all_to_all(values, axes, split_axis=0, concat_axis=0, tiled=True)  7.31 us
    pallas_call x1, Pallas kernels, on_device(): pl.pallas_call(functools.partial(prepare_kernel, cap, cap_back), in_specs...  7.2 us
    pallas_call x1, Pallas kernels, on_device(): pl.pallas_call(last_kernel, grid=(steps,), in_specs=head_specs, out_specs...  5.38 us
  transfers between devices with their start and end apart: 1, of which 0 were waited for; matrix products, arithmetic and copies ran while one was open for 0% of the time, Pallas kernels for 7%

commit v1 on v0

v1 whole, which is shorter than its diff:
```python
import functools

import jax
import jax.numpy as jnp
from jax import lax
from jax.experimental import pallas as pl
from jax.experimental.pallas import tpu as pltpu
from jax.sharding import PartitionSpec as P

root_half = 0.7071067811865476
LANES = 128
HIGH = 256
PAIR = 512
BLOCKS_IN_GROUP = 8
SLOT_ROWS = 8
MIB = 1024 * 1024

bf16 = jnp.bfloat16
f32 = jnp.float32
i32 = jnp.int32


def mm(a, b):
    return jnp.dot(a, b, preferred_element_type=f32)


def mm_nt(a, b):
    return lax.dot_general(a, b, (((1,), (1,)), ((), ())), preferred_element_type=f32)


def silu_of_half(u):
    return u + u * jnp.tanh(u)


def half_weight(ref):
    return ref[...] * bf16(0.5)


def lane(shape):
    return lax.broadcasted_iota(i32, shape, 1)


def one_hot_rows(high):
    at = lane(high.shape).astype(f32)
    parts = [jnp.where(high == at + k * LANES, f32(1), f32(0)).astype(bf16) for k in range(HIGH // LANES)]
    return jnp.concatenate(parts, axis=1)


def on_diagonal(values):
    row = lax.broadcasted_iota(i32, values.shape, 0)
    return jnp.where(row == lane(values.shape), values, f32(0)).astype(bf16)


def columns_of(rows):
    ones = jnp.ones((LANES, LANES), bf16)
    stacked = jnp.concatenate([on_diagonal(jnp.broadcast_to(r.astype(f32), (LANES, LANES))) for r in rows], axis=0)
    wide = mm(stacked, ones)
    return [wide[k * LANES : (k + 1) * LANES] for k in range(len(rows))]


def rows_of(column):
    return mm(jnp.ones((LANES, LANES), bf16), on_diagonal(column))


def swap_halves(v):
    return pltpu.roll(v, v.shape[1] // 2, 1)


def pick_group(wide, group, count):
    picked = wide[:, :LANES]
    for m in range(1, count):
        picked = jnp.where(group == m, wide[:, m * LANES : (m + 1) * LANES], picked)
    return picked


def residual_rows(x, inner_half, outer_half):
    hidden = silu_of_half(mm(x, inner_half)).astype(bf16)
    return ((x.astype(f32) + silu_of_half(mm(hidden, outer_half))) * root_half).astype(bf16)


def project_pair(inner_rows, down_t):
    zero = jnp.zeros_like(down_t)
    left = jnp.concatenate([down_t, zero], axis=0)
    right = jnp.concatenate([zero, down_t], axis=0)
    u = mm_nt(inner_rows[:HIGH], left) + mm_nt(inner_rows[HIGH:], right)
    return silu_of_half(u).astype(bf16)


def pick_sends(send_ref, pick_ref, low_ref, first, last):
    cap = send_ref.shape[1]
    half_cap = cap // 2
    pack = LANES // half_cap
    for base in range(first, last, pack):
        highs = []
        lows = []
        for o in range(base, base + pack, LANES // cap):
            row = jnp.concatenate([send_ref[o + k : o + k + 1, :] for k in range(LANES // cap)], axis=1)
            high, low = columns_of([row & (HIGH - 1), row >> 8])
            highs.append(high)
            lows.append(low)
        high = jnp.concatenate(highs, axis=0)
        low = jnp.concatenate(lows, axis=0)
        rows = slice(base * half_cap, (base + pack) * half_cap)
        for side in range(2):
            at = [slice(k * cap + side * half_cap, k * cap + (side + 1) * half_cap) for k in range(pack)]
            pick_ref[side, rows, :] = one_hot_rows(jnp.concatenate([high[t] for t in at], axis=0))
            low_ref[side, rows, :] = jnp.concatenate([low[t] for t in at], axis=0).astype(i32)


def write_payload(pick_ref, low_ref, table_ref, payload_ref):
    groups = table_ref.shape[1] // LANES
    table = table_ref[...]
    low_half = lane((HIGH, LANES)) < LANES // 2
    for base in range(0, payload_ref.shape[0], HIGH):
        sides = []
        for side in range(2):
            wide = mm(pick_ref[side, base : base + HIGH, :], table)
            low = low_ref[side, base : base + HIGH, :]
            picked = pick_group(wide, low >> 1, groups)
            sides.append(jnp.where((low & 1) == side, picked, swap_halves(picked)))
        payload_ref[base : base + HIGH, :] = jnp.where(low_half, sides[0], sides[1]).astype(bf16)


class Fetch:
    def __init__(self, sems, pairs):
        self.copies = [pltpu.make_async_copy(src, dst, sems.at[k]) for k, (src, dst) in enumerate(pairs)]
        for copy in self.copies:
            copy.start()

    def wait(self, *which):
        for k in which or range(len(self.copies)):
            self.copies[k].wait()


def row_chunks(ref):
    return [slice(base, base + PAIR) for base in range(0, ref.shape[0], PAIR)]


def first_kernel(
    layer,
    x_hbm,
    send_hbm,
    inner_hbm,
    outer_hbm,
    down_hbm,
    out_hbm,
    payload_ref,
    x_ref,
    send_ref,
    inner_ref,
    outer_ref,
    down_ref,
    out_ref,
    table_ref,
    pick_ref,
    low_ref,
    sems,
    out_sems,
):
    rows_half = x_ref.shape[0] // 2
    fetch = Fetch(
        sems,
        [
            (send_hbm, send_ref),
            (inner_hbm.at[layer], inner_ref),
            (outer_hbm.at[layer], outer_ref),
            (down_hbm.at[layer], down_ref),
            (x_hbm.at[0:rows_half], x_ref.at[0:rows_half]),
            (x_hbm.at[rows_half : 2 * rows_half], x_ref.at[rows_half : 2 * rows_half]),
        ],
    )
    fetch.wait(0)
    pick_sends(send_ref, pick_ref, low_ref, 0, send_ref.shape[0])
    fetch.wait(1, 2, 3, 4)
    inner_half, outer_half, down_half = half_weight(inner_ref), half_weight(outer_ref), half_weight(down_ref)
    for k, c in enumerate(row_chunks(x_ref)):
        if c.start == rows_half:
            fetch.wait(5)
        rows = residual_rows(x_ref[c, :], inner_half, outer_half)
        out_ref[c, :] = rows
        table_ref[:, k * LANES : (k + 1) * LANES] = project_pair(rows, down_half)
    store = Fetch(out_sems, [(out_ref, out_hbm)])
    write_payload(pick_ref, low_ref, table_ref, payload_ref)
    store.wait()


def gather_messages(incoming_ref, return_pick_ref, return_low_ref, message_ref):
    slots = incoming_ref.shape[0]
    low_half = lane((slots, LANES)) < LANES // 2
    upper = jnp.where(low_half, 0, 1)
    groups = message_ref.shape[1] // LANES
    pieces = []
    for g in range(return_low_ref.shape[0]):
        m, side = divmod(g, 2)
        both = incoming_ref[:, m * LANES : (m + 1) * LANES].astype(f32)
        other = swap_halves(both)
        spread = jnp.where(low_half, both, other) if side == 0 else jnp.where(low_half, other, both)
        low = return_low_ref[g]
        pieces.append(
            jnp.concatenate(
                [jnp.where(low == 2 * k + upper, spread, f32(0)).astype(bf16) for k in range(groups)], axis=1
            )
        )
    message_ref[...] = mm(return_pick_ref[...], jnp.concatenate(pieces, axis=0)).astype(bf16)


def join_rows(inner, message, up_half):
    zero = jnp.zeros_like(up_half)
    u = jnp.concatenate(
        [
            mm(message, jnp.concatenate([up_half, zero], axis=0)),
            mm(message, jnp.concatenate([zero, up_half], axis=0)),
        ],
        axis=0,
    )
    return ((inner.astype(f32) + silu_of_half(u)) * root_half).astype(bf16)


def middle_kernel(
    layer,
    incoming_ref,
    return_pick_ref,
    return_low_ref,
    x_ref,
    up_ref,
    post_inner_ref,
    post_outer_ref,
    pick_ref,
    low_ref,
    inner_ref,
    outer_ref,
    down_ref,
    out_ref,
    payload_ref,
    message_ref,
    table_ref,
):
    gather_messages(incoming_ref, return_pick_ref, return_low_ref, message_ref)
    up_half = half_weight(up_ref.at[layer])
    post_inner_half, post_outer_half = half_weight(post_inner_ref.at[layer]), half_weight(post_outer_ref.at[layer])
    inner_half, outer_half = half_weight(inner_ref.at[layer + 1]), half_weight(outer_ref.at[layer + 1])
    down_half = half_weight(down_ref.at[layer + 1])
    for k, c in enumerate(row_chunks(x_ref)):
        joined = join_rows(x_ref[c, :], message_ref[:, k * LANES : (k + 1) * LANES], up_half)
        state = residual_rows(joined, post_inner_half, post_outer_half)
        rows = residual_rows(state, inner_half, outer_half)
        out_ref[c, :] = rows
        table_ref[:, k * LANES : (k + 1) * LANES] = project_pair(rows, down_half)
    write_payload(pick_ref, low_ref, table_ref, payload_ref)


def last_kernel(
    layer,
    incoming_ref,
    return_pick_ref,
    return_low_ref,
    x_ref,
    up_ref,
    post_inner_ref,
    post_outer_ref,
    out_hbm,
    out_ref,
    message_ref,
    out_sems,
):
    gather_messages(incoming_ref, return_pick_ref, return_low_ref, message_ref)
    up_half = half_weight(up_ref.at[layer])
    post_inner_half, post_outer_half = half_weight(post_inner_ref.at[layer]), half_weight(post_outer_ref.at[layer])
    chunks = row_chunks(x_ref)
    stores = []
    for half in range(2):
        part = range(half * len(chunks) // 2, (half + 1) * len(chunks) // 2)
        for k in part:
            c = chunks[k]
            joined = join_rows(x_ref[c, :], message_ref[:, k * LANES : (k + 1) * LANES], up_half)
            out_ref[c, :] = residual_rows(joined, post_inner_half, post_outer_half)
        rows = slice(part[0] * PAIR, (part[-1] + 1) * PAIR)
        store = pltpu.make_async_copy(out_ref.at[rows], out_hbm.at[rows], out_sems.at[half])
        store.start()
        stores.append(store)
    for store in stores:
        store.wait()


def prepare_kernel(
    cap,
    cap_back,
    counts_ref,
    source_ref,
    target_ref,
    return_ref,
    send_ref,
    basis_hbm,
    bilinear_hbm,
    basis_out,
    source_out,
    weight_hbm,
    target_pick_hbm,
    target_low_hbm,
    return_pick_hbm,
    return_low_hbm,
    send_pick_hbm,
    send_low_hbm,
    basis_ref,
    bilinear_ref,
    weight_out,
    target_pick_out,
    target_low_out,
    return_pick_out,
    return_low_out,
    send_pick_out,
    send_low_out,
    high_ref,
    sems,
    out_sems,
):
    fetch = Fetch(sems, [(basis_hbm, basis_ref), (bilinear_hbm, bilinear_ref)])
    prepare_returns(cap_back, return_ref, return_pick_out, return_low_out, high_ref)
    pick_sends(send_ref, send_pick_out, send_low_out, 0, send_ref.shape[0])
    prepare_slots(cap, cap_back, counts_ref, source_ref, target_ref, source_out, target_pick_out, target_low_out, basis_ref.shape)
    fetch.wait()
    spread_weight(bilinear_ref, weight_out)
    stores = Fetch(
        out_sems,
        [
            (weight_out, weight_hbm),
            (target_pick_out, target_pick_hbm),
            (target_low_out, target_low_hbm),
            (return_pick_out, return_pick_hbm),
            (return_low_out, return_low_hbm),
            (send_pick_out, send_pick_hbm),
            (send_low_out, send_low_hbm),
        ],
    )
    turn_basis(basis_ref, basis_out)
    stores.wait()


def turn_basis(basis_ref, basis_out):
    blocks, width, span = basis_ref.shape
    sph = span // width
    groups = blocks // BLOCKS_IN_GROUP
    side_blocks = LANES // width
    to = lax.broadcasted_iota(i32, (span, span), 0)
    order = jnp.where(lane((span, span)) == (to % width) * sph + to // width, f32(1), f32(0)).astype(bf16)
    for g in range(groups):
        rows = jnp.concatenate(
            [
                basis_ref[g * side_blocks : (g + 1) * side_blocks].reshape(LANES, span),
                basis_ref[blocks // 2 + g * side_blocks : blocks // 2 + (g + 1) * side_blocks].reshape(LANES, span),
            ],
            axis=0,
        )
        basis_out[g] = mm_nt(order, rows).astype(bf16)


def spread_weight(bilinear_ref, weight_out):
    layers, trip, depth = bilinear_ref.shape
    zero = jnp.zeros((trip, LANES), bf16)
    for layer in range(layers):
        for k in range(0, depth // trip, 2):
            pair = jnp.transpose(bilinear_ref[layer, :, k * trip : (k + 2) * trip].astype(f32))
            both = jnp.concatenate([pair, pair], axis=1).astype(bf16)
            for j in range(2):
                w = both[j * trip : (j + 1) * trip]
                base = (k + j) * 2 * trip
                weight_out[layer, base : base + trip, :] = jnp.concatenate([w, zero], axis=1)
                weight_out[layer, base + trip : base + 2 * trip, :] = jnp.concatenate([zero, w], axis=1)


def prepare_slots(cap, cap_back, counts_ref, source_ref, target_ref, source_out, target_pick_out, target_low_out, basis_shape):
    blocks, width, _ = basis_shape
    groups = blocks // BLOCKS_IN_GROUP
    chunks = source_ref.shape[1] // LANES
    half_cap = cap // 2
    for chunk in range(chunks):
        side, g = divmod(chunk, groups)
        cols = slice(chunk * LANES, (chunk + 1) * LANES)
        s = source_ref[:, cols]
        rho = (s // cap) * half_cap + s % half_cap
        half = (s // half_cap) % 2
        row = target_ref[:, cols]
        picks, codes, lows = columns_of(
            [rho & (HIGH - 1), (rho >> 8) * 2 + (half ^ side), (row % cap_back) // SLOT_ROWS]
        )
        rows = slice(side * LANES, (side + 1) * LANES)
        source_out[g, rows, :] = (picks + codes * HIGH).astype(i32)
        target_low_out[cols, :] = lows.astype(i32)
    count = counts_ref[0]
    highs = target_pick_out.shape[0]
    for chunk in range(chunks):
        cols = slice(chunk * LANES, (chunk + 1) * LANES)
        row = target_ref[:, cols]
        high = (row // cap_back) * SLOT_ROWS + row % SLOT_ROWS
        live = (lane(row.shape) + chunk * LANES) // width < count
        high = jnp.broadcast_to(jnp.where(live, high, -1), (LANES, LANES))
        for h in range(highs // LANES):
            at = lax.broadcasted_iota(i32, (LANES, LANES), 0) + h * LANES
            target_pick_out[h * LANES : (h + 1) * LANES, cols] = jnp.where(high == at, f32(1), f32(0)).astype(bf16)


def prepare_returns(cap_back, return_ref, return_pick_out, return_low_out, high_ref):
    parts = cap_back // SLOT_ROWS
    owners_in = LANES // cap_back
    for chunk in range(return_ref.shape[1] // LANES):
        row = return_ref[:, chunk * LANES : (chunk + 1) * LANES]
        high, low = columns_of([row & (HIGH - 1), row >> 8])
        low = low.astype(i32)
        for o in range(owners_in):
            for g in range(parts):
                to = slice((chunk * owners_in + o) * SLOT_ROWS, (chunk * owners_in + o + 1) * SLOT_ROWS)
                at = slice((o * parts + g) * SLOT_ROWS, (o * parts + g + 1) * SLOT_ROWS)
                return_low_out[g, to, :] = low[at]
                high_ref[g, to, :] = high[at]
    slots = return_low_out.shape[1]
    for g in range(parts):
        for chunk in range(slots // LANES):
            high = rows_of(high_ref[g, chunk * LANES : (chunk + 1) * LANES, :])
            cols = slice(g * slots + chunk * LANES, g * slots + (chunk + 1) * LANES)
            for h in range(HIGH // LANES):
                at = (lax.broadcasted_iota(i32, (LANES, LANES), 0) + h * LANES).astype(f32)
                return_pick_out[h * LANES : (h + 1) * LANES, cols] = jnp.where(high == at, f32(1), f32(0)).astype(bf16)


def block_diagonal(kept, width):
    half_blocks = BLOCKS_IN_GROUP // 2
    zero = jnp.zeros((width, LANES), bf16)
    columns = []
    for j in range(half_blocks):
        pieces = []
        for side in range(2):
            for k in range(half_blocks):
                base = side * LANES + k * width
                pieces.append(kept[base : base + width] if k == j else zero)
        columns.append(jnp.concatenate(pieces, axis=0))
    return jnp.concatenate(columns, axis=1)


def owner_kernel(
    layer,
    arrived_ref,
    source_ref,
    basis_ref,
    weight_hbm,
    target_low_hbm,
    target_pick_hbm,
    out_ref,
    weight_ref,
    target_low_ref,
    target_pick_ref,
    kept_ref,
    lhs_ref,
    spread_ref,
    sems,
):
    fetch = Fetch(
        sems, [(weight_hbm.at[layer], weight_ref), (target_low_hbm, target_low_ref), (target_pick_hbm, target_pick_ref)]
    )
    groups, span, group_rows = basis_ref.shape
    half_blocks = BLOCKS_IN_GROUP // 2
    width = LANES // half_blocks
    sph = span // width
    tables = arrived_ref.shape[0] // HIGH
    table = jnp.concatenate([arrived_ref[m * HIGH : (m + 1) * HIGH, :] for m in range(tables)], axis=1)
    shape = (group_rows, LANES)
    own_half = (lax.broadcasted_iota(i32, shape, 0) >= LANES) == (lane(shape) >= LANES // 2)
    for g in range(groups):
        source = source_ref[g]
        wide = mm(one_hot_rows((source & (HIGH - 1)).astype(f32)), table)
        code = source >> 8
        picked = pick_group(wide, code >> 1, tables)
        turned = jnp.where((code & 1) == 1, swap_halves(picked), picked)
        kept_ref[g] = jnp.where(own_half, turned, f32(0)).astype(bf16)
    for g in range(groups):
        contracted = mm(basis_ref[g], block_diagonal(kept_ref[g], width)).astype(bf16)
        for j in range(half_blocks):
            rows = slice(g * LANES + j * width, g * LANES + (j + 1) * width)
            for k in range(sph):
                lhs_ref[rows, k * LANES : (k + 1) * LANES] = contracted[k * width : (k + 1) * width, j * LANES : (j + 1) * LANES]
    fetch.wait()
    half_rows = lhs_ref.shape[0]
    chunk = min(half_rows, PAIR)
    upper = jnp.where(lane((chunk, LANES)) < LANES // 2, 0, 1)
    lane_groups = spread_ref.shape[1] // LANES
    for base in range(0, half_rows, chunk):
        partial = mm(lhs_ref[base : base + chunk, :], weight_ref[...])
        for side in range(2):
            rows = slice(side * half_rows + base, side * half_rows + base + chunk)
            low = target_low_ref[rows, :]
            values = partial[:, side * LANES : (side + 1) * LANES]
            for m in range(lane_groups):
                spread_ref[rows, m * LANES : (m + 1) * LANES] = jnp.where(low == 2 * m + upper, values, f32(0)).astype(bf16)
    out_ref[...] = mm(target_pick_ref[...], spread_ref[...]).astype(bf16)


IN_HBM = pl.BlockSpec(memory_space=pl.ANY)
IN_VMEM = pl.BlockSpec(memory_space=pltpu.VMEM)
IN_SMEM = pl.BlockSpec(memory_space=pltpu.SMEM)


def run(kernel, name, in_specs, outs, scratch, operands, mib=32, flops=10**9):
    out_specs, out_shapes = zip(*outs)
    return pl.pallas_call(
        kernel,
        in_specs=in_specs,
        out_specs=list(out_specs),
        out_shape=list(out_shapes),
        scratch_shapes=scratch,
        compiler_params=pltpu.CompilerParams(vmem_limit_bytes=mib * MIB),
        cost_estimate=pl.CostEstimate(flops=flops, bytes_accessed=8 * 10**6, transcendentals=0),
        name=name,
    )(*operands)


def like(array):
    return pltpu.VMEM(array.shape, array.dtype)


def of_layer(array):
    return pltpu.VMEM(array.shape[1:], array.dtype)


def on_device(
    bond_states,
    block_counts,
    send_rows,
    source_slots,
    target_slots,
    return_rows,
    angular_basis,
    pre_inner,
    pre_outer,
    down_proj,
    bilinear,
    up_proj,
    post_inner,
    post_outer,
):
    axes = ("bond", "atom")
    peers = lax.axis_size("bond") * lax.axis_size("atom")
    rows, depth = bond_states.shape
    blocks, width, span = angular_basis.shape
    layers, _, trip = down_proj.shape
    cap = send_rows.shape[2]
    returns = return_rows.shape[1]
    cap_back = returns // peers
    lookup = peers * cap // 2
    slots = peers * SLOT_ROWS
    slot_lanes = cap_back // SLOT_ROWS * trip
    groups = blocks // BLOCKS_IN_GROUP
    group_rows = BLOCKS_IN_GROUP * width
    send = send_rows.reshape(peers, cap)
    down_t = jnp.swapaxes(down_proj, 1, 2)
    bilinear_t = jnp.swapaxes(bilinear, 1, 2)
    shape_of = jax.ShapeDtypeStruct
    row_shape = shape_of((rows, depth), bf16)
    payload_shape = shape_of((lookup, LANES), bf16)
    pick_shape = (2, lookup, HIGH)
    low_shape = (2, lookup, LANES)
    wide_scratch = pltpu.VMEM((HIGH, rows // HIGH * trip), bf16)
    row_scratch = pltpu.VMEM((rows, depth), bf16)

    def exchange(values, per_peer):
        values = values.reshape(peers, per_peer, values.shape[1])
        got = lax.all_to_all(values, axes, split_axis=0, concat_axis=0, tiled=True)
        return got.reshape(peers * per_peer, values.shape[2])

    inner, payload = run(
        functools.partial(first_kernel, 0),
        "first",
        [IN_HBM] * 5,
        [(IN_HBM, row_shape), (IN_VMEM, payload_shape)],
        [row_scratch, like(send), of_layer(pre_inner), of_layer(pre_outer), of_layer(down_t), row_scratch, wide_scratch]
        + [pltpu.VMEM(pick_shape, bf16), pltpu.VMEM(low_shape, i32)]
        + [pltpu.SemaphoreType.DMA((6,)), pltpu.SemaphoreType.DMA((1,))],
        (bond_states, send, pre_inner, pre_outer, down_t),
        mib=60,
    )

    kept_shapes = [shape_of((groups, span, group_rows), bf16), shape_of((groups, group_rows, LANES), i32)]
    stored_shapes = [
        shape_of((layers, bilinear.shape[1] * 2, 2 * LANES), bf16),
        shape_of((slots, blocks * width), bf16),
        shape_of((blocks * width, LANES), i32),
        shape_of((HIGH, returns), bf16),
        shape_of((cap_back // SLOT_ROWS, slots, LANES), i32),
        shape_of(pick_shape, bf16),
        shape_of(low_shape, i32),
    ]
    basis, source, weight, target_pick, target_low, return_pick, return_low, send_pick, send_low = run(
        functools.partial(prepare_kernel, cap, cap_back),
        "prepare",
        [IN_SMEM] + [IN_VMEM] * 4 + [IN_HBM] * 2,
        [(IN_VMEM, shape) for shape in kept_shapes] + [(IN_HBM, shape) for shape in stored_shapes],
        [like(angular_basis), like(bilinear_t)]
        + [like(shape) for shape in stored_shapes]
        + [pltpu.VMEM((cap_back // SLOT_ROWS, slots, LANES), f32)]
        + [pltpu.SemaphoreType.DMA((2,)), pltpu.SemaphoreType.DMA((len(stored_shapes),))],
        (block_counts, source_slots, target_slots, return_rows, send, angular_basis, bilinear_t),
        mib=48,
        flops=4 * 10**9,
    )

    out = None
    for layer in range(layers):
        arrived = exchange(payload, cap // 2)
        (slot_sums,) = run(
            functools.partial(owner_kernel, layer),
            "owner",
            [IN_VMEM] * 3 + [IN_HBM] * 3,
            [(IN_VMEM, shape_of((slots, slot_lanes), bf16))],
            [of_layer(weight), like(target_low), like(target_pick)]
            + [pltpu.VMEM((groups, group_rows, LANES), bf16)]
            + [pltpu.VMEM((blocks * width // 2, weight.shape[1]), bf16), pltpu.VMEM((blocks * width, slot_lanes), bf16)]
            + [pltpu.SemaphoreType.DMA((3,))],
            (arrived, source, basis, weight, target_low, target_pick),
        )
        incoming = exchange(slot_sums, SLOT_ROWS)
        head = (incoming, return_pick, return_low, inner, up_proj, post_inner, post_outer)
        if layer + 1 < layers:
            inner, payload = run(
                functools.partial(middle_kernel, layer),
                "middle",
                [IN_VMEM] * 12,
                [(IN_VMEM, row_shape), (IN_VMEM, payload_shape)],
                [wide_scratch, wide_scratch],
                head + (send_pick, send_low, pre_inner, pre_outer, down_t),
            )
        else:
            (out,) = run(
                functools.partial(last_kernel, layer),
                "last",
                [IN_VMEM] * 7,
                [(IN_HBM, row_shape)],
                [row_scratch, wide_scratch, pltpu.SemaphoreType.DMA((2,))],
                head,
            )
    return out


def solution(mesh):
    split = ("bond", "atom")
    in_specs = (
        P(split, None),
        P(split),
        P(split, None, None),
        P(split, None),
        P(split, None),
        P(split, None),
        P(split, None, None),
    ) + (P(),) * 7
    return jax.shard_map(on_device, mesh=mesh, in_specs=in_specs, out_specs=P(split, None), check_vma=False)
```

time: 108 us -> 88.5 us (0.82)
  Pallas kernels: 53.1 us -> 34.4 us
  blocking collectives: 36.2 us -> 35 us
  waiting for transfers between devices: 0.01 us -> 1.2 us
    pallas_call x6, Pallas kernels: 53.1 us -> 34.4 us  [run(): pl.pallas_call(kernel, in_specs=in_specs, out_specs=list(out_specs), out_...]
    all_to_all x1, waiting for transfers between devices: 0.01 us -> 1.2 us  [exchange(): got = lax.all_to_all(values, axes, split_axis=0, concat_axis=0, tiled=True)]
    all_to_all x3, blocking collectives: 36.2 us -> 35 us  [exchange(): got = lax.all_to_all(values, axes, split_axis=0, concat_axis=0, tiled=True)]
    unnamed x48 -> x46, local copies, waits for them, and re-layouts: 10.2 us -> 9.2 us
  transfers between devices with their start and end apart: 1 -> 1, of which waited for: 0 -> 1; matrix products, arithmetic and copies ran while one was open for 0% -> 0% of each run, Pallas kernels for 7% -> 6%
where the time goes in v1:
time: 88.5 us; the launch traced here: 88.1 us
  blocking collectives  35 us (40%)
  Pallas kernels  34.4 us (39%)
  local copies, waits for them, and re-layouts  9.2 us (10%)
  starting transfers between devices  7.3 us (8%)
  waiting for transfers between devices  1.2 us (1%)
  between operations  1.04 us (1%)
    all_to_all x3, blocking collectives, exchange(): got = lax.all_to_all(values, axes, split_axis=0, concat_axis=0, tiled=True)  35 us
    pallas_call x6, Pallas kernels, run(): pl.pallas_call(kernel, in_specs=in_specs, out_specs=list(out_specs), out_...  34.4 us
    unnamed x46, local copies, waits for them, and re-layouts  9.2 us
    all_to_all x1, starting transfers between devices, exchange(): got = lax.all_to_all(values, axes, split_axis=0, concat_axis=0, tiled=True)  7.3 us
  transfers between devices with their start and end apart: 1, of which 1 were waited for; matrix products, arithmetic and copies ran while one was open for 0% of the time, Pallas kernels for 6%

profile of v1, /device:TPU:0, one launch (start us, length us, event | category | flops | bytes accessed | tf_op | source)
XLA Modules:
  0.0 88.1 jit_solution(9628262884631095370)
XLA Ops:
  0.0 0.0 copy-start.18
  0.0 0.0 copy-start.20
  0.0 0.0 copy-start.21
  0.0 0.0 copy-start.22
  0.0 7.3 %first.1 = (bf16[2048,512]{1,0:T(8,128)(2,1)}, bf16[1024,128]{1,0:T(8,128)(2,1)}) custom-call(bf16[2048,512]{1,0:T(8,128)(2,1)} %x_hbm.1, s32[32,64]{1,0:T(8,128)} %bitcast.20, bf16[2,512,512]{2,1,0:T(8,128)(2,1)} %inner_ref.1, bf16[2,512,512]{2,1,0:T(8,128)(2,1)} %outer_ref.1, bf16[2,64,512]{2,1,0:T(8,128)(2,1)} %bitcast.13), custom_call_target="tpu_custom_call" | custom-call | flops 1000000000 | bytes 8000000 | tf_op jit(solution)/shard_map/first/pallas_call | solution.py:503
  7.3 7.3 %all-to-all-start = ((bf16[32,32,128]{2,1,0:T(8,128)(2,1)}), bf16[32,32,128]{2,1,0:T(8,128)(2,1)S(1)}, u32[]{:S(2)}, u32[]{:S(2)}) async-start(bf16[32,32,128]{2,1,0:T(8,128)(2,1)} %bitcast.23), calls=%async_computation | async-start | bytes 524288 | tf_op jit(solution)/shard_map/all_to_all | solution.py:565
  15.3 0.0 copy-done.18
  15.3 0.0 copy-done.20
  15.3 0.0 copy-done.21
  15.3 0.0 copy-done.22
  15.3 0.0 copy-start.19
  15.3 0.9 %copy-done.19 = bf16[2,1024,64]{1,2,0:T(8,128)(2,1)S(1)} copy-done((bf16[2,1024,64]{1,2,0:T(8,128)(2,1)S(1)}, bf16[2,1024,64]{1,2,0:T(8,128)(2,1)}, u32[]{:S(2)}) %copy-start.19) | copy-done | bytes 262168
  16.3 5.2 %prepare.1 = (bf16[8,512,256]{2,1,0:T(8,128)(2,1)}, s32[8,256,128]{2,1,0:T(8,128)S(1)}, bf16[2,2048,256]{2,1,0:T(8,128)(2,1)}, bf16[256,2048]{1,0:T(8,128)(2,1)S...) custom-call(s32[1]{0:T(128)S(6)} %copy.15.counts_ref, ...), custom_call_target="tpu_custom_call" | custom-call | flops 4000000000 | bytes 8000000 | tf_op jit(solution)/shard_map/prepare/pallas_call | solution.py:503
  21.5 0.0 copy-start.9
  21.5 0.8 copy-done.9
  22.3 0.0 copy-start.11
  22.3 0.8 copy-done.11
  23.1 0.0 copy-start.13
  23.1 1.0 %copy-done.13 = bf16[2,1024,256]{2,1,0:T(8,128)(2,1)} copy-done((bf16[2,1024,256]{2,1,0:T(8,128)(2,1)}, bf16[2,1024,256]{2,1,0:T(8,128)(2,1)S(1)}, u32[]{:S(2)}) %copy-start.13) | copy-done | bytes 1048600
  24.1 1.2 %all-to-all-done = bf16[32,32,128]{2,1,0:T(8,128)(2,1)S(1)} async-done(((bf16[32,32,128]{2,1,0:T(8,128)(2,1)}), bf16[32,32,128]{2,1,0:T(8,128)(2,1)S(1)}, u32[]{:S(2)}, u32[]{:S(2)}) %all-to-all-start) | async-done | bytes 262176 | tf_op jit(solution)/shard_map/all_to_all | solution.py:565
  25.3 0.0 copy-start
  25.3 1.6 %copy-done = bf16[8,512,256]{2,1,0:T(8,128)(2,1)S(1)} copy-done((bf16[8,512,256]{2,1,0:T(8,128)(2,1)S(1)}, bf16[8,512,256]{2,1,0:T(8,128)(2,1)}, u32[]{:S(2)}) %copy-start) | copy-done | bytes 2097176
  26.9 0.0 copy-start.2
  26.9 1.6 %copy-done.2 = bf16[2,2048,256]{2,1,0:T(8,128)(2,1)S(1)} copy-done((bf16[2,2048,256]{2,1,0:T(8,128)(2,1)S(1)}, bf16[2,2048,256]{2,1,0:T(8,128)(2,1)}, u32[]{:S(2)}) %copy-start.2) | copy-done | bytes 2097176
  28.5 0.0 copy-start.4
  28.5 0.0 copy-start.5
  28.5 0.0 copy-start.6
  28.5 0.0 copy-start.7
  28.5 0.0 copy-start.8
  28.5 0.0 copy-start.10
  28.5 0.0 copy-start.12
  28.5 0.0 copy-start.16
  28.5 0.0 copy-start.17
  28.5 4.5 %owner.2 = bf16[256,256]{1,0:T(8,128)(2,1)S(1)} custom-call(bf16[1024,128]{1,0:T(8,128)(2,1)S(1)} %bitcast.11, s32[8,256,128]{2,1,0:T(8,128)S(1)} %get-tuple-element.19.source_ref, bf16[8,512,256]{2,1,0:T(8,128)(2,1)S(1)} %copy-done, bf16[2,2048,256]{2,1,0:T(8,128)(2,1)S(1)} %copy-done.2, s32[2048,128]{1,0:T(8,128)S(1)} %get-tuple-element.22.target_low_hbm, ...), custom_call_target="tpu_custom_call" | custom-call | flops 1000000000 | bytes 8000000 | tf_op jit(solution)/shard_map/owner/pallas_call | solution.py:503
  33.0 12.2 %all_to_all.20 = bf16[32,8,256]{2,1,0:T(8,128)(2,1)S(1)} all-to-all(bf16[32,8,256]{2,1,0:T(8,128)(2,1)S(1)} %bitcast.17), channel_id=1, replica_groups=mesh['bond'=4,'atom'=8] {'bond','atom'}, dimensions={0} | all-to-all | bytes 262144 | tf_op jit(solution)/shard_map/all_to_all | solution.py:565
  45.2 0.0 copy-done.4
  45.2 0.0 copy-done.5
  45.2 0.0 copy-done.6
  45.2 0.0 copy-done.7
  45.2 0.0 copy-done.8
  45.2 0.0 copy-done.10
  45.2 0.0 copy-done.12
  45.2 0.0 copy-done.16
  45.2 0.0 copy-done.17
  45.2 0.0 copy-start.14
  45.3 1.2 %copy-done.14 = bf16[2,1024,256]{2,1,0:T(8,128)(2,1)S(1)} copy-done((bf16[2,1024,256]{2,1,0:T(8,128)(2,1)S(1)}, bf16[2,1024,256]{2,1,0:T(8,128)(2,1)}, u32[]{:S(2)}) %copy-start.14) | copy-done | bytes 1048600
  46.5 0.0 copy-start.15
  46.5 1.2 %copy-done.15 = s32[2,1024,128]{2,1,0:T(8,128)S(1)} copy-done((s32[2,1024,128]{2,1,0:T(8,128)S(1)}, s32[2,1024,128]{2,1,0:T(8,128)}, u32[]{:S(2)}) %copy-start.15) | copy-done | bytes 1048600
  47.7 0.0 copy-start.1
  47.7 0.0 copy-start.3
  47.7 7.9 %middle.1 = (bf16[2048,512]{1,0:T(8,128)(2,1)S(1)}, bf16[1024,128]{1,0:T(8,128)(2,1)S(1)}) custom-call(bf16[256,256]{1,0:T(8,128)(2,1)S(1)} %bitcast.15, bf16[256,1024]{1,0:T(8,128)(2,1)S(1)} %copy-done.10, s32[4,256,128]{2,1,0:T(8,128)S(1)} %copy-done.12, bf16[2048,512]{1,0:T(8,128)(2,1)S(1)} %copy-done.8, bf16[2,64,512]{2,1,0:T(8,128)(2,1)S(1)} %copy-done.17, ...), custom_call_target="tpu_custom_call" | custom-call | flops 1000000000 | bytes 8000000 | tf_op jit(solution)/shard_map/middle/pallas_call | solution.py:503
  55.6 12.9 %all_to_all.21 = bf16[32,32,128]{2,1,0:T(8,128)(2,1)S(1)} all-to-all(bf16[32,32,128]{2,1,0:T(8,128)(2,1)S(1)} %bitcast.19), channel_id=1, replica_groups=mesh['bond'=4,'atom'=8] {'bond','atom'}, dimensions={0} | all-to-all | bytes 524288 | tf_op jit(solution)/shard_map/all_to_all | solution.py:565
  68.5 0.0 copy-done.1
  68.5 0.0 copy-done.3
  68.5 4.5 %owner.3 = bf16[256,256]{1,0:T(8,128)(2,1)S(1)} custom-call(bf16[1024,128]{1,0:T(8,128)(2,1)S(1)} %bitcast.12, s32[8,256,128]{2,1,0:T(8,128)S(1)} %get-tuple-element.19.source_ref, bf16[8,512,256]{2,1,0:T(8,128)(2,1)S(1)} %copy-done.1, bf16[2,2048,256]{2,1,0:T(8,128)(2,1)S(1)} %copy-done.3, s32[2048,128]{1,0:T(8,128)S(1)} %get-tuple-element.22.target_low_hbm, ...), custom_call_target="tpu_custom_call" | custom-call | flops 1000000000 | bytes 8000000 | tf_op jit(solution)/shard_map/owner/pallas_call | solution.py:503
  73.0 9.9 %all_to_all.22 = bf16[32,8,256]{2,1,0:T(8,128)(2,1)S(1)} all-to-all(bf16[32,8,256]{2,1,0:T(8,128)(2,1)S(1)} %bitcast.16), channel_id=1, replica_groups=mesh['bond'=4,'atom'=8] {'bond','atom'}, dimensions={0} | all-to-all | bytes 262144 | tf_op jit(solution)/shard_map/all_to_all | solution.py:565
  82.9 5.0 %last.1 = bf16[2048,512]{1,0:T(8,128)(2,1)} custom-call(bf16[256,256]{1,0:T(8,128)(2,1)S(1)} %bitcast.18, bf16[256,1024]{1,0:T(8,128)(2,1)S(1)} %copy-done.10, s32[4,256,128]{2,1,0:T(8,128)S(1)} %copy-done.12, bf16[2048,512]{1,0:T(8,128)(2,1)S(1)} %get-tuple-element.30.x_ref, bf16[2,64,512]{2,1,0:T(8,128)(2,1)S(1)} %copy-done.17, ...), custom_call_target="tpu_custom_call" | custom-call | flops 1000000000 | bytes 8000000 | tf_op jit(solution)/shard_map/last/pallas_call | solution.py:503
Async XLA Ops:
  0.0 15.3 %copy-start.18 = (s32[1,32,64]{2,1,0:T(8,128)S(1)}, s32[1,32,64]{2,1,0:T(8,128)}, u32[]{:S(2)}) copy-start(s32[1,32,64]{2,1,0:T(8,128)} %param.16) | copy-start | bytes 24580
  0.0 15.3 %copy-start.20 = (s32[1,2048]{1,0:T(1,128)S(1)}, s32[1,2048]{1,0:T(1,128)}, u32[]{:S(2)}) copy-start(s32[1,2048]{1,0:T(1,128)} %source_ref.1) | copy-start | bytes 24580
  0.0 15.3 %copy-start.21 = (s32[1,2048]{1,0:T(1,128)S(1)}, s32[1,2048]{1,0:T(1,128)}, u32[]{:S(2)}) copy-start(s32[1,2048]{1,0:T(1,128)} %target_ref.1) | copy-start | bytes 24580
  0.0 15.3 %copy-start.22 = (s32[1,1024]{1,0:T(1,128)S(1)}, s32[1,1024]{1,0:T(1,128)}, u32[]{:S(2)}) copy-start(s32[1,1024]{1,0:T(1,128)} %return_ref.1) | copy-start | bytes 12292
  7.3 18.0 %all-to-all-start = ((bf16[32,32,128]{2,1,0:T(8,128)(2,1)}), bf16[32,32,128]{2,1,0:T(8,128)(2,1)S(1)}, u32[]{:S(2)}, u32[]{:S(2)}) async-start(bf16[32,32,128]{2,1,0:T(8,128)(2,1)} %bitcast.23), calls=%async_computation | async-start | bytes 524288 | tf_op jit(solution)/shard_map/all_to_all | solution.py:565
  15.3 1.0 %copy-start.19 = (bf16[2,1024,64]{1,2,0:T(8,128)(2,1)S(1)}, bf16[2,1024,64]{1,2,0:T(8,128)(2,1)}, u32[]{:S(2)}) copy-start(bf16[2,1024,64]{1,2,0:T(8,128)(2,1)} %param.24) | copy-start | bytes 786436
  21.5 0.8 copy-start.9
  22.3 0.8 copy-start.11
  23.1 1.0 %copy-start.13 = (bf16[2,1024,256]{2,1,0:T(8,128)(2,1)}, bf16[2,1024,256]{2,1,0:T(8,128)(2,1)S(1)}, u32[]{:S(2)}) copy-start(bf16[2,1024,256]{2,1,0:T(8,128)(2,1)S(1)} %get-tuple-element.27.pick_ref) | copy-start | bytes 3145732
  25.3 1.6 %copy-start = (bf16[8,512,256]{2,1,0:T(8,128)(2,1)S(1)}, bf16[8,512,256]{2,1,0:T(8,128)(2,1)}, u32[]{:S(2)}) copy-start(bf16[8,512,256]{2,1,0:T(8,128)(2,1)} %get-tuple-element.20.basis_ref) | copy-start | bytes 6291460
  26.9 1.6 %copy-start.2 = (bf16[2,2048,256]{2,1,0:T(8,128)(2,1)S(1)}, bf16[2,2048,256]{2,1,0:T(8,128)(2,1)}, u32[]{:S(2)}) copy-start(bf16[2,2048,256]{2,1,0:T(8,128)(2,1)} %get-tuple-element.21.weight_hbm) | copy-start | bytes 6291460
  28.5 16.7 %copy-start.4 = (bf16[2,512,512]{2,1,0:T(8,128)(2,1)S(1)}, bf16[2,512,512]{2,1,0:T(8,128)(2,1)}, u32[]{:S(2)}) copy-start(bf16[2,512,512]{2,1,0:T(8,128)(2,1)} %inner_ref.1) | copy-start | bytes 3145732
  28.5 16.7 %copy-start.5 = (bf16[2,512,512]{2,1,0:T(8,128)(2,1)S(1)}, bf16[2,512,512]{2,1,0:T(8,128)(2,1)}, u32[]{:S(2)}) copy-start(bf16[2,512,512]{2,1,0:T(8,128)(2,1)} %outer_ref.1) | copy-start | bytes 3145732
  28.5 16.7 %copy-start.6 = (bf16[2,512,512]{2,1,0:T(8,128)(2,1)S(1)}, bf16[2,512,512]{2,1,0:T(8,128)(2,1)}, u32[]{:S(2)}) copy-start(bf16[2,512,512]{2,1,0:T(8,128)(2,1)} %post_inner_ref.3) | copy-start | bytes 3145732
  28.5 16.7 %copy-start.7 = (bf16[2,512,512]{2,1,0:T(8,128)(2,1)S(1)}, bf16[2,512,512]{2,1,0:T(8,128)(2,1)}, u32[]{:S(2)}) copy-start(bf16[2,512,512]{2,1,0:T(8,128)(2,1)} %post_outer_ref.3) | copy-start | bytes 3145732
  28.5 16.7 %copy-start.8 = (bf16[2048,512]{1,0:T(8,128)(2,1)S(1)}, bf16[2048,512]{1,0:T(8,128)(2,1)}, u32[]{:S(2)}) copy-start(bf16[2048,512]{1,0:T(8,128)(2,1)} %get-tuple-element.26.x_ref) | copy-start | bytes 6291460
  28.5 16.7 %copy-start.10 = (bf16[256,1024]{1,0:T(8,128)(2,1)S(1)}, bf16[256,1024]{1,0:T(8,128)(2,1)}, u32[]{:S(2)}) copy-start(bf16[256,1024]{1,0:T(8,128)(2,1)} %copy-done.9) | copy-start | bytes 1572868
  28.5 16.7 %copy-start.12 = (s32[4,256,128]{2,1,0:T(8,128)S(1)}, s32[4,256,128]{2,1,0:T(8,128)}, u32[]{:S(2)}) copy-start(s32[4,256,128]{2,1,0:T(8,128)} %copy-done.11) | copy-start | bytes 1572868
  28.5 16.7 %copy-start.16 = (bf16[2,512,64]{1,2,0:T(8,128)(2,1)S(1)}, bf16[2,512,64]{1,2,0:T(8,128)(2,1)}, u32[]{:S(2)}) copy-start(bf16[2,512,64]{1,2,0:T(8,128)(2,1)} %param.23) | copy-start | bytes 393220
  28.5 16.7 %copy-start.17 = (bf16[2,64,512]{2,1,0:T(8,128)(2,1)S(1)}, bf16[2,64,512]{2,1,0:T(8,128)(2,1)}, u32[]{:S(2)}) copy-start(bf16[2,64,512]{2,1,0:T(8,128)(2,1)} %up_ref.3) | copy-start | bytes 393220
  45.2 1.2 %copy-start.14 = (bf16[2,1024,256]{2,1,0:T(8,128)(2,1)S(1)}, bf16[2,1024,256]{2,1,0:T(8,128)(2,1)}, u32[]{:S(2)}) copy-start(bf16[2,1024,256]{2,1,0:T(8,128)(2,1)} %copy-done.13) | copy-start | bytes 3145732
  46.5 1.2 %copy-start.15 = (s32[2,1024,128]{2,1,0:T(8,128)S(1)}, s32[2,1024,128]{2,1,0:T(8,128)}, u32[]{:S(2)}) copy-start(s32[2,1024,128]{2,1,0:T(8,128)} %get-tuple-element.28.low_ref) | copy-start | bytes 3145732
  47.7 20.8 %copy-start.1 = (bf16[8,512,256]{2,1,0:T(8,128)(2,1)S(1)}, bf16[8,512,256]{2,1,0:T(8,128)(2,1)}, u32[]{:S(2)}) copy-start(bf16[8,512,256]{2,1,0:T(8,128)(2,1)} %get-tuple-element.20.basis_ref) | copy-start | bytes 6291460
  47.7 20.8 %copy-start.3 = (bf16[2,2048,256]{2,1,0:T(8,128)(2,1)S(1)}, bf16[2,2048,256]{2,1,0:T(8,128)(2,1)}, u32[]{:S(2)}) copy-start(bf16[2,2048,256]{2,1,0:T(8,128)(2,1)} %get-tuple-element.21.weight_hbm) | copy-start | bytes 6291460

commit v2 on v1

v2 whole, which is shorter than its diff:
```python
import functools

import jax
import jax.numpy as jnp
from jax import lax
from jax.experimental import pallas as pl
from jax.experimental.pallas import tpu as pltpu
from jax.sharding import PartitionSpec as P

root_half = 0.7071067811865476
LANES = 128
HIGH = 256
PAIR = 512
BLOCKS_IN_GROUP = 8
SLOT_ROWS = 8
MIB = 1024 * 1024

bf16 = jnp.bfloat16
f32 = jnp.float32
i32 = jnp.int32


def mm(a, b):
    return jnp.dot(a, b, preferred_element_type=f32)


def mm_nt(a, b):
    return lax.dot_general(a, b, (((1,), (1,)), ((), ())), preferred_element_type=f32)


def silu_of_half(u):
    return u + u * jnp.tanh(u)


def half_weight(ref):
    return ref[...] * bf16(0.5)


def lane(shape):
    return lax.broadcasted_iota(i32, shape, 1)


def one_hot_rows(high):
    at = lane(high.shape).astype(f32)
    parts = [jnp.where(high == at + k * LANES, f32(1), f32(0)).astype(bf16) for k in range(HIGH // LANES)]
    return jnp.concatenate(parts, axis=1)


def on_diagonal(values):
    row = lax.broadcasted_iota(i32, values.shape, 0)
    return jnp.where(row == lane(values.shape), values, f32(0)).astype(bf16)


def columns_of(rows):
    ones = jnp.ones((LANES, LANES), bf16)
    stacked = jnp.concatenate([on_diagonal(jnp.broadcast_to(r.astype(f32), (LANES, LANES))) for r in rows], axis=0)
    wide = mm(stacked, ones)
    return [wide[k * LANES : (k + 1) * LANES] for k in range(len(rows))]


def rows_of(column):
    return mm(jnp.ones((LANES, LANES), bf16), on_diagonal(column))


def swap_halves(v):
    return pltpu.roll(v, v.shape[1] // 2, 1)


def pick_group(wide, group, count):
    picked = wide[:, :LANES]
    for m in range(1, count):
        picked = jnp.where(group == m, wide[:, m * LANES : (m + 1) * LANES], picked)
    return picked


def residual_rows(x, inner_half, outer_half):
    hidden = silu_of_half(mm(x, inner_half)).astype(bf16)
    return ((x.astype(f32) + silu_of_half(mm(hidden, outer_half))) * root_half).astype(bf16)


def project_pair(inner_rows, down_t):
    zero = jnp.zeros_like(down_t)
    left = jnp.concatenate([down_t, zero], axis=0)
    right = jnp.concatenate([zero, down_t], axis=0)
    u = mm_nt(inner_rows[:HIGH], left) + mm_nt(inner_rows[HIGH:], right)
    return silu_of_half(u).astype(bf16)


def pack_sends(send_ref, packed_ref):
    owners, cap = send_ref.shape
    half_cap = cap // 2
    pack = LANES // half_cap
    for base in range(0, owners, pack):
        packed = []
        for o in range(base, base + pack, LANES // cap):
            row = jnp.concatenate([send_ref[o + k : o + k + 1, :] for k in range(LANES // cap)], axis=1)
            high, low = columns_of([row & (HIGH - 1), row >> 8])
            packed.append((high + low * HIGH).astype(i32))
        packed = jnp.concatenate(packed, axis=0)
        rows = slice(base * half_cap, (base + pack) * half_cap)
        for side in range(2):
            at = [slice(k * cap + side * half_cap, k * cap + (side + 1) * half_cap) for k in range(pack)]
            packed_ref[side, rows, :] = jnp.concatenate([packed[t] for t in at], axis=0)


def write_payload(packed_ref, table_ref, payload_ref):
    groups = table_ref.shape[1] // LANES
    table = table_ref[...]
    low_half = lane((HIGH, LANES)) < LANES // 2
    for base in range(0, payload_ref.shape[0], HIGH):
        sides = []
        for side in range(2):
            packed = packed_ref[side, base : base + HIGH, :]
            wide = mm(one_hot_rows((packed & (HIGH - 1)).astype(f32)), table)
            low = packed >> 8
            picked = pick_group(wide, low >> 1, groups)
            sides.append(jnp.where((low & 1) == side, picked, swap_halves(picked)))
        payload_ref[base : base + HIGH, :] = jnp.where(low_half, sides[0], sides[1]).astype(bf16)


class Fetch:
    def __init__(self, sems, pairs):
        self.copies = [pltpu.make_async_copy(src, dst, sems.at[k]) for k, (src, dst) in enumerate(pairs)]
        for copy in self.copies:
            copy.start()

    def wait(self, *which):
        for k in which or range(len(self.copies)):
            self.copies[k].wait()


def row_chunks(ref):
    return [slice(base, base + PAIR) for base in range(0, ref.shape[0], PAIR)]


def first_kernel(
    layers,
    x_hbm,
    send_hbm,
    inner_hbm,
    outer_hbm,
    down_hbm,
    post_inner_hbm,
    post_outer_hbm,
    out_hbm,
    payload_ref,
    *rest,
):
    layer = 0
    split = [(w, n) for w in (post_inner_hbm, post_outer_hbm) for n in range(layers)]
    split += [(w, n) for w in (inner_hbm, outer_hbm) for n in range(1, layers)]
    split_out = rest[: len(split)]
    (
        x_ref,
        send_ref,
        inner_ref,
        outer_ref,
        down_ref,
        out_ref,
        table_ref,
        packed_ref,
        split_ref,
        sems,
        out_sems,
        load_sems,
        split_sems,
    ) = rest[len(split) :]
    rows_half = x_ref.shape[0] // 2
    fetch = Fetch(
        sems,
        [
            (send_hbm, send_ref),
            (inner_hbm.at[layer], inner_ref),
            (outer_hbm.at[layer], outer_ref),
            (down_hbm.at[layer], down_ref),
            (x_hbm.at[0:rows_half], x_ref.at[0:rows_half]),
            (x_hbm.at[rows_half : 2 * rows_half], x_ref.at[rows_half : 2 * rows_half]),
        ],
    )
    fetch.wait(0)
    pack_sends(send_ref, packed_ref)
    fetch.wait(1, 2, 3, 4)
    loads = Fetch(load_sems, [(w.at[n], split_ref.at[k]) for k, (w, n) in enumerate(split)])
    inner_half, outer_half, down_half = half_weight(inner_ref), half_weight(outer_ref), half_weight(down_ref)
    halves = [slice(0, rows_half), slice(rows_half, 2 * rows_half)]
    stores = [pltpu.make_async_copy(out_ref.at[h], out_hbm.at[h], out_sems.at[k]) for k, h in enumerate(halves)]
    for k, c in enumerate(row_chunks(x_ref)):
        if c.start == rows_half:
            stores[0].start()
            fetch.wait(5)
            loads.wait()
            copies = Fetch(split_sems, [(split_ref.at[n], to) for n, to in enumerate(split_out)])
        rows = residual_rows(x_ref[c, :], inner_half, outer_half)
        out_ref[c, :] = rows
        table_ref[:, k * LANES : (k + 1) * LANES] = project_pair(rows, down_half)
    stores[1].start()
    write_payload(packed_ref, table_ref, payload_ref)
    for store in stores:
        store.wait()
    copies.wait()


def one_hot_columns(high_ref, slab, first, count, n):
    rows = [high_ref[slab, first + k : first + k + 1, :] for k in range(n // LANES)]
    high = jnp.concatenate(rows, axis=1).astype(f32)
    at = lax.broadcasted_iota(i32, (count, high.shape[1]), 0).astype(f32)
    return jnp.where(high == at, f32(1), f32(0)).astype(bf16)


def gather_messages(incoming_ref, return_low_ref, message_ref):
    slots = incoming_ref.shape[0]
    low_half = lane((slots, LANES)) < LANES // 2
    upper = jnp.where(low_half, 0, 1)
    groups = message_ref.shape[1] // LANES
    total = None
    parts = return_low_ref.shape[0] - 1
    for g in range(parts):
        m, side = divmod(g, 2)
        both = incoming_ref[:, m * LANES : (m + 1) * LANES].astype(f32)
        other = swap_halves(both)
        spread = jnp.where(low_half, both, other) if side == 0 else jnp.where(low_half, other, both)
        low = return_low_ref[g]
        piece = jnp.concatenate(
            [jnp.where(low == 2 * k + upper, spread, f32(0)).astype(bf16) for k in range(groups)], axis=1
        )
        part = mm(one_hot_columns(return_low_ref, parts, g * (slots // LANES), HIGH, slots), piece)
        total = part if total is None else total + part
    message_ref[...] = total.astype(bf16)


def join_rows(inner, message, up_half):
    zero = jnp.zeros_like(up_half)
    u = jnp.concatenate(
        [
            mm(message, jnp.concatenate([up_half, zero], axis=0)),
            mm(message, jnp.concatenate([zero, up_half], axis=0)),
        ],
        axis=0,
    )
    return ((inner.astype(f32) + silu_of_half(u)) * root_half).astype(bf16)


def middle_kernel(
    layer,
    incoming_ref,
    return_low_ref,
    x_hbm,
    up_ref,
    post_inner_ref,
    post_outer_ref,
    send_ref,
    down_ref,
    inner_ref,
    outer_ref,
    out_hbm,
    payload_ref,
    x_ref,
    out_ref,
    message_ref,
    table_ref,
    packed_ref,
    sems,
    out_sems,
):
    rows_half = x_ref.shape[0] // 2
    halves = [slice(0, rows_half), slice(rows_half, 2 * rows_half)]
    fetch = Fetch(sems, [(x_hbm.at[h], x_ref.at[h]) for h in halves])
    stores = [pltpu.make_async_copy(out_ref.at[h], out_hbm.at[h], out_sems.at[k]) for k, h in enumerate(halves)]
    gather_messages(incoming_ref, return_low_ref, message_ref)
    up_half = half_weight(up_ref.at[layer])
    post_inner_half, post_outer_half = half_weight(post_inner_ref), half_weight(post_outer_ref)
    inner_half, outer_half = half_weight(inner_ref), half_weight(outer_ref)
    down_half = half_weight(down_ref.at[layer + 1])
    fetch.wait(0)
    for k, c in enumerate(row_chunks(x_ref)):
        if c.start == rows_half:
            stores[0].start()
            fetch.wait(1)
        joined = join_rows(x_ref[c, :], message_ref[:, k * LANES : (k + 1) * LANES], up_half)
        state = residual_rows(joined, post_inner_half, post_outer_half)
        rows = residual_rows(state, inner_half, outer_half)
        out_ref[c, :] = rows
        table_ref[:, k * LANES : (k + 1) * LANES] = project_pair(rows, down_half)
    stores[1].start()
    pack_sends(send_ref, packed_ref)
    write_payload(packed_ref, table_ref, payload_ref)
    for store in stores:
        store.wait()


def last_kernel(
    layer,
    incoming_ref,
    return_low_ref,
    x_ref,
    up_ref,
    post_inner_ref,
    post_outer_ref,
    out_hbm,
    out_ref,
    message_ref,
    out_sems,
):
    gather_messages(incoming_ref, return_low_ref, message_ref)
    up_half = half_weight(up_ref.at[layer])
    post_inner_half, post_outer_half = half_weight(post_inner_ref), half_weight(post_outer_ref)
    chunks = row_chunks(x_ref)
    stores = []
    count = len(chunks)
    bounds = [0, count // 2, count - 1, count]
    for n in range(3):
        part = range(bounds[n], bounds[n + 1])
        for k in part:
            c = chunks[k]
            joined = join_rows(x_ref[c, :], message_ref[:, k * LANES : (k + 1) * LANES], up_half)
            out_ref[c, :] = residual_rows(joined, post_inner_half, post_outer_half)
        rows = slice(part[0] * PAIR, (part[-1] + 1) * PAIR)
        store = pltpu.make_async_copy(out_ref.at[rows], out_hbm.at[rows], out_sems.at[n])
        store.start()
        stores.append(store)
    for store in stores:
        store.wait()


def prepare_kernel(
    cap,
    cap_back,
    counts_ref,
    source_ref,
    target_ref,
    return_ref,
    basis_hbm,
    bilinear_hbm,
    basis_out,
    source_out,
    return_low_out,
    basis_ref,
    bilinear_ref,
    high_ref,
    sems,
):
    fetch = Fetch(sems, [(basis_hbm, basis_ref), (bilinear_hbm, bilinear_ref)])
    prepare_returns(cap_back, return_ref, return_low_out, high_ref)
    prepare_slots(cap, cap_back, counts_ref, source_ref, target_ref, source_out, basis_ref.shape)
    fetch.wait()
    turn_basis(basis_ref, basis_out)
    layers, trip, depth = bilinear_ref.shape
    width = basis_out.shape[2]
    slab = basis_out.shape[0] - 1
    for layer in range(layers):
        for piece in range(depth // width):
            base = (layer * (depth // width) + piece) * trip
            basis_out[slab, base : base + trip, :] = bilinear_ref[layer, :, piece * width : (piece + 1) * width]


def turn_basis(basis_ref, basis_out):
    blocks, width, span = basis_ref.shape
    sph = span // width
    groups = blocks // BLOCKS_IN_GROUP
    side_blocks = LANES // width
    to = lax.broadcasted_iota(i32, (span, span), 0)
    order = jnp.where(lane((span, span)) == (to % width) * sph + to // width, f32(1), f32(0)).astype(bf16)
    for g in range(groups):
        rows = jnp.concatenate(
            [
                basis_ref[g * side_blocks : (g + 1) * side_blocks].reshape(LANES, span),
                basis_ref[blocks // 2 + g * side_blocks : blocks // 2 + (g + 1) * side_blocks].reshape(LANES, span),
            ],
            axis=0,
        )
        basis_out[g] = mm_nt(order, rows).astype(bf16)


def spread_weight(basis_ref, layer, trip, weight_out):
    slab, _, width = basis_ref.shape
    slab -= 1
    depth = weight_out.shape[0] // 2
    zero = jnp.zeros((trip, LANES), bf16)
    for k in range(0, depth // trip, 2):
        piece, at = divmod(k * trip, width)
        base = (layer * (depth // width) + piece) * trip
        pair = jnp.transpose(basis_ref[slab, base : base + trip, at : at + LANES].astype(f32))
        both = jnp.concatenate([pair, pair], axis=1).astype(bf16)
        for j in range(2):
            w = both[j * trip : (j + 1) * trip]
            base = (k + j) * 2 * trip
            weight_out[base : base + trip, :] = jnp.concatenate([w, zero], axis=1)
            weight_out[base + trip : base + 2 * trip, :] = jnp.concatenate([zero, w], axis=1)


def prepare_slots(cap, cap_back, counts_ref, source_ref, target_ref, source_out, basis_shape):
    blocks, width, _ = basis_shape
    groups = blocks // BLOCKS_IN_GROUP
    chunks = source_ref.shape[1] // LANES
    half_cap = cap // 2
    for chunk in range(chunks):
        side, g = divmod(chunk, groups)
        cols = slice(chunk * LANES, (chunk + 1) * LANES)
        s = source_ref[:, cols]
        rho = (s // cap) * half_cap + s % half_cap
        half = (s // half_cap) % 2
        row = target_ref[:, cols]
        picks, codes, lows = columns_of(
            [rho & (HIGH - 1), (rho >> 8) * 2 + (half ^ side), (row % cap_back) // SLOT_ROWS]
        )
        rows = slice(side * LANES, (side + 1) * LANES)
        source_out[g, rows, :] = (picks + codes * HIGH).astype(i32) + lows.astype(i32) * (HIGH * HIGH)
        live = (lane(row.shape) + chunk * LANES) // width < counts_ref[0]
        high = jnp.where(live, (row // cap_back) * SLOT_ROWS + row % SLOT_ROWS, -1)
        source_out[groups, chunk : chunk + 1, :] = high


def prepare_returns(cap_back, return_ref, return_low_out, high_ref):
    parts = cap_back // SLOT_ROWS
    owners_in = LANES // cap_back
    for chunk in range(return_ref.shape[1] // LANES):
        row = return_ref[:, chunk * LANES : (chunk + 1) * LANES]
        high, low = columns_of([row & (HIGH - 1), row >> 8])
        low = low.astype(i32)
        for o in range(owners_in):
            for g in range(parts):
                to = slice((chunk * owners_in + o) * SLOT_ROWS, (chunk * owners_in + o + 1) * SLOT_ROWS)
                at = slice((o * parts + g) * SLOT_ROWS, (o * parts + g + 1) * SLOT_ROWS)
                return_low_out[g, to, :] = low[at]
                high_ref[g, to, :] = high[at]
    slots = return_low_out.shape[1]
    for g in range(parts):
        for chunk in range(slots // LANES):
            high = rows_of(high_ref[g, chunk * LANES : (chunk + 1) * LANES, :])
            at = g * (slots // LANES) + chunk
            return_low_out[parts, at : at + 1, :] = high[0:1, :].astype(i32)


def block_diagonal(kept, width):
    half_blocks = BLOCKS_IN_GROUP // 2
    zero = jnp.zeros((width, LANES), bf16)
    columns = []
    for j in range(half_blocks):
        pieces = []
        for side in range(2):
            for k in range(half_blocks):
                base = side * LANES + k * width
                pieces.append(kept[base : base + width] if k == j else zero)
        columns.append(jnp.concatenate(pieces, axis=0))
    return jnp.concatenate(columns, axis=1)


def owner_kernel(
    layer,
    arrived_ref,
    source_ref,
    basis_ref,
    out_ref,
    weight_ref,
    kept_ref,
    lhs_ref,
    spread_ref,
):
    slabs, span, group_rows = basis_ref.shape
    groups = slabs - 1
    spread_weight(basis_ref, layer, LANES // 2, weight_ref)
    half_blocks = BLOCKS_IN_GROUP // 2
    width = LANES // half_blocks
    sph = span // width
    tables = arrived_ref.shape[0] // HIGH
    table = jnp.concatenate([arrived_ref[m * HIGH : (m + 1) * HIGH, :] for m in range(tables)], axis=1)
    shape = (group_rows, LANES)
    own_half = (lax.broadcasted_iota(i32, shape, 0) >= LANES) == (lane(shape) >= LANES // 2)
    for g in range(groups):
        source = source_ref[g]
        wide = mm(one_hot_rows((source & (HIGH - 1)).astype(f32)), table)
        code = (source >> 8) & (HIGH - 1)
        picked = pick_group(wide, code >> 1, tables)
        turned = jnp.where((code & 1) == 1, swap_halves(picked), picked)
        kept_ref[g] = jnp.where(own_half, turned, f32(0)).astype(bf16)
    for g in range(groups):
        contracted = mm(basis_ref[g], block_diagonal(kept_ref[g], width)).astype(bf16)
        for j in range(half_blocks):
            rows = slice(g * LANES + j * width, g * LANES + (j + 1) * width)
            for k in range(sph):
                lhs_ref[rows, k * LANES : (k + 1) * LANES] = contracted[k * width : (k + 1) * width, j * LANES : (j + 1) * LANES]
    half_rows = lhs_ref.shape[0]
    chunk = min(half_rows, PAIR)
    upper = jnp.where(lane((chunk, LANES)) < LANES // 2, 0, 1)
    lane_groups = spread_ref.shape[1] // LANES
    for base in range(0, half_rows, chunk):
        partial = mm(lhs_ref[base : base + chunk, :], weight_ref[...])
        for side in range(2):
            rows = slice(side * half_rows + base, side * half_rows + base + chunk)
            at = slice(side * LANES, (side + 1) * LANES)
            first = base // LANES
            low = jnp.concatenate([source_ref[g, at, :] >> 16 for g in range(first, first + chunk // LANES)], axis=0)
            values = partial[:, at]
            for m in range(lane_groups):
                spread_ref[rows, m * LANES : (m + 1) * LANES] = jnp.where(low == 2 * m + upper, values, f32(0)).astype(bf16)
    total = None
    for base in range(0, spread_ref.shape[0], chunk):
        part = mm(one_hot_columns(source_ref, groups, base // LANES, out_ref.shape[0], chunk), spread_ref[base : base + chunk, :])
        total = part if total is None else total + part
    out_ref[...] = total.astype(bf16)


IN_HBM = pl.BlockSpec(memory_space=pl.ANY)
IN_VMEM = pl.BlockSpec(memory_space=pltpu.VMEM)
IN_SMEM = pl.BlockSpec(memory_space=pltpu.SMEM)


def run(kernel, name, in_specs, outs, scratch, operands, mib=32, flops=10**9):
    out_specs, out_shapes = zip(*outs)
    return pl.pallas_call(
        kernel,
        in_specs=in_specs,
        out_specs=list(out_specs),
        out_shape=list(out_shapes),
        scratch_shapes=scratch,
        compiler_params=pltpu.CompilerParams(vmem_limit_bytes=mib * MIB),
        cost_estimate=pl.CostEstimate(flops=flops, bytes_accessed=8 * 10**6, transcendentals=0),
        name=name,
    )(*operands)


def like(array):
    return pltpu.VMEM(array.shape, array.dtype)


def of_layer(array):
    return pltpu.VMEM(array.shape[1:], array.dtype)


def on_device(
    bond_states,
    block_counts,
    send_rows,
    source_slots,
    target_slots,
    return_rows,
    angular_basis,
    pre_inner,
    pre_outer,
    down_proj,
    bilinear,
    up_proj,
    post_inner,
    post_outer,
):
    axes = ("bond", "atom")
    peers = lax.axis_size("bond") * lax.axis_size("atom")
    rows, depth = bond_states.shape
    blocks, width, span = angular_basis.shape
    layers, _, trip = down_proj.shape
    cap = send_rows.shape[2]
    returns = return_rows.shape[1]
    cap_back = returns // peers
    lookup = peers * cap // 2
    slots = peers * SLOT_ROWS
    slot_lanes = cap_back // SLOT_ROWS * trip
    groups = blocks // BLOCKS_IN_GROUP
    group_rows = BLOCKS_IN_GROUP * width
    send = send_rows.reshape(peers, cap)
    down_t = jnp.swapaxes(down_proj, 1, 2)
    bilinear_t = jnp.swapaxes(bilinear, 1, 2)
    shape_of = jax.ShapeDtypeStruct
    row_shape = shape_of((rows, depth), bf16)
    payload_shape = shape_of((lookup, LANES), bf16)
    packed_scratch = pltpu.VMEM((2, lookup, LANES), i32)
    wide_scratch = pltpu.VMEM((HIGH, rows // HIGH * trip), bf16)
    row_scratch = pltpu.VMEM((rows, depth), bf16)

    def exchange(values, per_peer):
        values = values.reshape(peers, per_peer, values.shape[1])
        got = lax.all_to_all(values, axes, split_axis=0, concat_axis=0, tiled=True)
        return got.reshape(peers * per_peer, values.shape[2])

    weight_shape = shape_of((depth, depth), bf16)
    splits = 2 * layers + 2 * (layers - 1)
    inner, payload, *weights = run(
        functools.partial(first_kernel, layers),
        "first",
        [IN_HBM] * 7,
        [(IN_HBM, row_shape), (IN_VMEM, payload_shape)] + [(IN_HBM, weight_shape)] * splits,
        [row_scratch, like(send), of_layer(pre_inner), of_layer(pre_outer), of_layer(down_t), row_scratch, wide_scratch]
        + [packed_scratch, pltpu.VMEM((splits, depth, depth), bf16)]
        + [pltpu.SemaphoreType.DMA((n,)) for n in (6, 2, splits, splits)],
        (bond_states, send, pre_inner, pre_outer, down_t, post_inner, post_outer),
        mib=60,
    )
    post_inners, post_outers = weights[:layers], weights[layers : 2 * layers]
    pre_inners = [None] + weights[2 * layers : 3 * layers - 1]
    pre_outers = [None] + weights[3 * layers - 1 :]

    parts = cap_back // SLOT_ROWS
    basis, source, return_low = run(
        functools.partial(prepare_kernel, cap, cap_back),
        "prepare",
        [IN_SMEM] + [IN_VMEM] * 3 + [IN_HBM] * 2,
        [
            (IN_VMEM, shape_of((groups + 1, span, group_rows), bf16)),
            (IN_VMEM, shape_of((groups + 1, group_rows, LANES), i32)),
            (IN_VMEM, shape_of((parts + 1, slots, LANES), i32)),
        ],
        [like(angular_basis), like(bilinear_t), pltpu.VMEM((parts, slots, LANES), f32), pltpu.SemaphoreType.DMA((2,))],
        (block_counts, source_slots, target_slots, return_rows, angular_basis, bilinear_t),
        flops=4 * 10**9,
    )

    out = None
    for layer in range(layers):
        arrived = exchange(payload, cap // 2)
        (slot_sums,) = run(
            functools.partial(owner_kernel, layer),
            "owner",
            [IN_VMEM] * 3,
            [(IN_VMEM, shape_of((slots, slot_lanes), bf16))],
            [
                pltpu.VMEM((bilinear.shape[1] * 2, 2 * LANES), bf16),
                pltpu.VMEM((groups, group_rows, LANES), bf16),
                pltpu.VMEM((blocks * width // 2, bilinear.shape[1] * 2), bf16),
                pltpu.VMEM((blocks * width, slot_lanes), bf16),
            ],
            (arrived, source, basis),
        )
        incoming = exchange(slot_sums, SLOT_ROWS)
        head = (incoming, return_low, inner, up_proj, post_inners[layer], post_outers[layer])
        if layer + 1 < layers:
            inner, payload = run(
                functools.partial(middle_kernel, layer),
                "middle",
                [IN_VMEM] * 2 + [IN_HBM] + [IN_VMEM] * 7,
                [(IN_HBM, row_shape), (IN_VMEM, payload_shape)],
                [row_scratch, row_scratch, wide_scratch, wide_scratch, packed_scratch]
                + [pltpu.SemaphoreType.DMA((2,)), pltpu.SemaphoreType.DMA((2,))],
                head + (send, down_t, pre_inners[layer + 1], pre_outers[layer + 1]),
                mib=49,
            )
        else:
            (out,) = run(
                functools.partial(last_kernel, layer),
                "last",
                [IN_VMEM] * 6,
                [(IN_HBM, row_shape)],
                [row_scratch, wide_scratch, pltpu.SemaphoreType.DMA((3,))],
                head,
            )
    return out


def solution(mesh):
    split = ("bond", "atom")
    in_specs = (
        P(split, None),
        P(split),
        P(split, None, None),
        P(split, None),
        P(split, None),
        P(split, None),
        P(split, None, None),
    ) + (P(),) * 7
    return jax.shard_map(on_device, mesh=mesh, in_specs=in_specs, out_specs=P(split, None), check_vma=False)
```

time: 88.5 us -> 82.1 us (0.928)
  local copies, waits for them, and re-layouts: 9.2 us -> 4.1 us
  blocking collectives: 35 us -> 32.7 us
  waiting for transfers between devices: 1.2 us -> 3.49 us
  Pallas kernels: 34.4 us -> 33 us
    unnamed x46 -> x34, local copies, waits for them, and re-layouts: 9.2 us -> 4.1 us
    all_to_all x1, waiting for transfers between devices: 1.2 us -> 3.49 us  [exchange(): got = lax.all_to_all(values, axes, split_axis=0, concat_axis=0, tiled=True)]
    all_to_all x3, blocking collectives: 35 us -> 32.7 us  [exchange(): got = lax.all_to_all(values, axes, split_axis=0, concat_axis=0, tiled=True)]
    pallas_call x6, Pallas kernels: 34.4 us -> 33 us  [run(): pl.pallas_call(kernel, in_specs=in_specs, out_specs=list(out_specs), out_...]
  transfers between devices with their start and end apart: 1 -> 1, of which waited for: 1 -> 1; matrix products, arithmetic and copies ran while one was open for 0% -> 0% of each run, Pallas kernels for 6% -> 3%
where the time goes in v2:
time: 82.1 us; the launch traced here: 81.7 us
  Pallas kernels  33 us (40%)
  blocking collectives  32.7 us (40%)
  starting transfers between devices  7.43 us (9%)
  local copies, waits for them, and re-layouts  4.1 us (5%)
  waiting for transfers between devices  3.49 us (4%)
  between operations  1 us (1%)
    pallas_call x6, Pallas kernels, run(): pl.pallas_call(kernel, in_specs=in_specs, out_specs=list(out_specs), out_...  33 us
    all_to_all x3, blocking collectives, exchange(): got = lax.all_to_all(values, axes, split_axis=0, concat_axis=0, tiled=True)  32.7 us
    all_to_all x1, starting transfers between devices, exchange(): got = lax.all_to_all(values, axes, split_axis=0, concat_axis=0, tiled=True)  7.43 us
    unnamed x34, local copies, waits for them, and re-layouts  4.1 us
    all_to_all x1, waiting for transfers between devices, exchange(): got = lax.all_to_all(values, axes, split_axis=0, concat_axis=0, tiled=True)  3.49 us
  transfers between devices with their start and end apart: 1, of which 1 were waited for; matrix products, arithmetic and copies ran while one was open for 0% of the time, Pallas kernels for 3%

profile of v2, /device:TPU:0, one launch (start us, length us, event | category | flops | bytes accessed | tf_op | source)
XLA Modules:
  0.0 81.7 jit_solution(3310427558685716977)
XLA Ops:
  0.0 0.0 copy-start.14
  0.0 0.0 copy-start.15
  0.0 7.2 %first.1 = (bf16[2048,512]{1,0:T(8,128)(2,1)}, bf16[1024,128]{1,0:T(8,128)(2,1)}, bf16[512,512]{1,0:T(8,128)(2,1)}, bf16[512,512]{1,0:T(8,128)(2,1)}, bf16[512,5...) custom-call(bf16[2048,512]{1,0:T(8,128)(2,1)} %x_hbm.1, ...), custom_call_target="tpu_custom_call" | custom-call | flops 1000000000 | bytes 8000000 | tf_op jit(solution)/shard_map/first/pallas_call | solution.py:510
  7.2 7.4 %all-to-all-start = ((bf16[32,32,128]{2,1,0:T(8,128)(2,1)}), bf16[32,32,128]{2,1,0:T(8,128)(2,1)}, u32[]{:S(2)}, u32[]{:S(2)}) async-start(bf16[32,32,128]{2,1,0:T(8,128)(2,1)} %bitcast.22), calls=%async_computation | async-start | bytes 524288 | tf_op jit(solution)/shard_map/all_to_all | solution.py:571
  15.3 0.0 copy-done.14
  15.3 0.0 copy-done.15
  15.3 0.0 copy-start.12
  15.3 1.6 %copy-done.12 = bf16[64,32,512]{2,1,0:T(8,128)(2,1)S(1)} copy-done((bf16[64,32,512]{2,1,0:T(8,128)(2,1)S(1)}, bf16[64,32,512]{2,1,0:T(8,128)(2,1)}, u32[]{:S(2)}) %copy-start.12) | copy-done | bytes 2097176
  16.9 0.0 copy-start.13
  16.9 0.9 %copy-done.13 = bf16[2,1024,64]{1,2,0:T(8,128)(2,1)S(1)} copy-done((bf16[2,1024,64]{1,2,0:T(8,128)(2,1)S(1)}, bf16[2,1024,64]{1,2,0:T(8,128)(2,1)}, u32[]{:S(2)}) %copy-start.13) | copy-done | bytes 262168
  17.8 0.0 copy-start.16
  17.8 0.7 copy-done.16
  18.5 2.4 %prepare.1 = (bf16[9,512,256]{2,1,0:T(8,128)(2,1)S(1)}, s32[9,256,128]{2,1,0:T(8,128)S(1)}, s32[5,256,128]{2,1,0:T(8,128)S(1)}) custom-call(s32[1]{0:T(128)S(6)} %copy.15.counts_ref, s32[1,2048]{1,0:T(1,128)S(1)} %copy-done.14, s32[1,2048]{1,0:T(1,128)S(1)} %copy-done.15, s32[1,1024]{1,0:T(1,128)S(1)} %copy-done.16, bf16[64,32,512]{2,1,0:T(8,128)(2,1)S(1)} %copy-done.12, ...), custom_call_target="tpu_custom_call" | custom-call | flops 4000000000 | bytes 8000000 | tf_op jit(solution)/shard_map/prepare/pallas_call | solution.py:510
  20.9 0.0 copy-start
  20.9 0.8 %copy-done = s32[5,256,128]{2,1,0:T(8,128)} copy-done((s32[5,256,128]{2,1,0:T(8,128)}, s32[5,256,128]{2,1,0:T(8,128)S(1)}, u32[]{:S(2)}) %copy-start) | copy-done | bytes 655384
  21.8 3.5 %all-to-all-done = bf16[32,32,128]{2,1,0:T(8,128)(2,1)} async-done(((bf16[32,32,128]{2,1,0:T(8,128)(2,1)}), bf16[32,32,128]{2,1,0:T(8,128)(2,1)}, u32[]{:S(2)}, u32[]{:S(2)}) %all-to-all-start) | async-done | bytes 262176 | tf_op jit(solution)/shard_map/all_to_all | solution.py:571
  25.2 0.0 copy-start.1
  25.3 0.0 copy-start.5
  25.3 0.0 copy-start.6
  25.3 0.0 copy-start.7
  25.3 0.0 copy-start.8
  25.3 0.0 copy-start.9
  25.3 0.0 copy-start.10
  25.3 0.0 copy-start.11
  25.3 5.1 %owner.2 = bf16[256,256]{1,0:T(8,128)(2,1)S(1)} custom-call(bf16[1024,128]{1,0:T(8,128)(2,1)} %bitcast.3.arrived_ref, s32[9,256,128]{2,1,0:T(8,128)S(1)} %get-tuple-element.19.source_ref, bf16[9,512,256]{2,1,0:T(8,128)(2,1)S(1)} %get-tuple-element.20.basis_ref), custom_call_target="tpu_custom_call" | custom-call | flops 1000000000 | bytes 8000000 | tf_op jit(solution)/shard_map/owner/pallas_call | solution.py:510
  30.4 9.9 %all_to_all.20 = bf16[32,8,256]{2,1,0:T(8,128)(2,1)S(1)} all-to-all(bf16[32,8,256]{2,1,0:T(8,128)(2,1)S(1)} %bitcast.17), channel_id=1, replica_groups=mesh['bond'=4,'atom'=8] {'bond','atom'}, dimensions={0} | all-to-all | bytes 262144 | tf_op jit(solution)/shard_map/all_to_all | solution.py:571
  40.3 0.0 copy-done.1
  40.3 0.0 copy-done.5
  40.3 0.0 copy-done.6
  40.3 0.0 copy-done.7
  40.3 0.0 copy-done.8
  40.3 0.0 copy-done.9
  40.3 0.0 copy-done.10
  40.3 0.0 copy-done.11
  40.4 9.4 %middle.1 = (bf16[2048,512]{1,0:T(8,128)(2,1)}, bf16[1024,128]{1,0:T(8,128)(2,1)S(1)}) custom-call(bf16[256,256]{1,0:T(8,128)(2,1)S(1)} %bitcast.14, s32[5,256,128]{2,1,0:T(8,128)S(1)} %copy-done.1, bf16[2048,512]{1,0:T(8,128)(2,1)} %get-tuple-element.22.x_hbm, bf16[2,64,512]{2,1,0:T(8,128)(2,1)S(1)} %copy-done.10, bf16[512,512]{1,0:T(8,128)(2,1)S(1)} %copy-done.5, ...), custom_call_target="tpu_custom_call" | custom-call | flops 1000000000 | bytes 8000000 | tf_op jit(solution)/shard_map/middle/pallas_call | solution.py:510
  49.8 12.9 %all_to_all.21 = bf16[32,32,128]{2,1,0:T(8,128)(2,1)S(1)} all-to-all(bf16[32,32,128]{2,1,0:T(8,128)(2,1)S(1)} %bitcast.18), channel_id=1, replica_groups=mesh['bond'=4,'atom'=8] {'bond','atom'}, dimensions={0} | all-to-all | bytes 524288 | tf_op jit(solution)/shard_map/all_to_all | solution.py:571
  62.7 0.0 copy-start.2
  62.7 0.0 copy-start.3
  62.7 0.0 copy-start.4
  62.7 3.9 %owner.3 = bf16[256,256]{1,0:T(8,128)(2,1)S(1)} custom-call(bf16[1024,128]{1,0:T(8,128)(2,1)S(1)} %bitcast.11, s32[9,256,128]{2,1,0:T(8,128)S(1)} %get-tuple-element.19.source_ref, bf16[9,512,256]{2,1,0:T(8,128)(2,1)S(1)} %get-tuple-element.20.basis_ref), custom_call_target="tpu_custom_call" | custom-call | flops 1000000000 | bytes 8000000 | tf_op jit(solution)/shard_map/owner/pallas_call | solution.py:510
  66.6 9.9 %all_to_all.22 = bf16[32,8,256]{2,1,0:T(8,128)(2,1)S(1)} all-to-all(bf16[32,8,256]{2,1,0:T(8,128)(2,1)S(1)} %bitcast.16), channel_id=1, replica_groups=mesh['bond'=4,'atom'=8] {'bond','atom'}, dimensions={0} | all-to-all | bytes 262144 | tf_op jit(solution)/shard_map/all_to_all | solution.py:571
  76.5 0.0 copy-done.2
  76.6 0.0 copy-done.3
  76.6 0.0 copy-done.4
  76.6 5.0 %last.1 = bf16[2048,512]{1,0:T(8,128)(2,1)} custom-call(bf16[256,256]{1,0:T(8,128)(2,1)S(1)} %bitcast.15, s32[5,256,128]{2,1,0:T(8,128)S(1)} %copy-done.1, bf16[2048,512]{1,0:T(8,128)(2,1)S(1)} %copy-done.2, bf16[2,64,512]{2,1,0:T(8,128)(2,1)S(1)} %copy-done.10, bf16[512,512]{1,0:T(8,128)(2,1)S(1)} %copy-done.3, bf16[512,512]{1,0:T(8,128)(2,1)S(1)} %copy-done.4), custom_call_target="tpu_custom_call" | custom-call | flops 1000000000 | bytes 8000000 | tf_op jit(solution)/shard_map/last/pallas_call | solution.py:510
Async XLA Ops:
  0.0 15.3 %copy-start.14 = (s32[1,2048]{1,0:T(1,128)S(1)}, s32[1,2048]{1,0:T(1,128)}, u32[]{:S(2)}) copy-start(s32[1,2048]{1,0:T(1,128)} %source_ref.1) | copy-start | bytes 24580
  0.0 15.3 %copy-start.15 = (s32[1,2048]{1,0:T(1,128)S(1)}, s32[1,2048]{1,0:T(1,128)}, u32[]{:S(2)}) copy-start(s32[1,2048]{1,0:T(1,128)} %target_ref.1) | copy-start | bytes 24580
  7.2 18.1 %all-to-all-start = ((bf16[32,32,128]{2,1,0:T(8,128)(2,1)}), bf16[32,32,128]{2,1,0:T(8,128)(2,1)}, u32[]{:S(2)}, u32[]{:S(2)}) async-start(bf16[32,32,128]{2,1,0:T(8,128)(2,1)} %bitcast.22), calls=%async_computation | async-start | bytes 524288 | tf_op jit(solution)/shard_map/all_to_all | solution.py:571
  15.3 1.6 %copy-start.12 = (bf16[64,32,512]{2,1,0:T(8,128)(2,1)S(1)}, bf16[64,32,512]{2,1,0:T(8,128)(2,1)}, u32[]{:S(2)}) copy-start(bf16[64,32,512]{2,1,0:T(8,128)(2,1)} %basis_hbm.1) | copy-start | bytes 6291460
  16.9 0.9 %copy-start.13 = (bf16[2,1024,64]{1,2,0:T(8,128)(2,1)S(1)}, bf16[2,1024,64]{1,2,0:T(8,128)(2,1)}, u32[]{:S(2)}) copy-start(bf16[2,1024,64]{1,2,0:T(8,128)(2,1)} %param.24) | copy-start | bytes 786436
  17.8 0.7 copy-start.16
  20.9 0.8 %copy-start = (s32[5,256,128]{2,1,0:T(8,128)}, s32[5,256,128]{2,1,0:T(8,128)S(1)}, u32[]{:S(2)}) copy-start(s32[5,256,128]{2,1,0:T(8,128)S(1)} %get-tuple-element.21.return_low_ref) | copy-start | bytes 1966084
  25.2 15.0 %copy-start.1 = (s32[5,256,128]{2,1,0:T(8,128)S(1)}, s32[5,256,128]{2,1,0:T(8,128)}, u32[]{:S(2)}) copy-start(s32[5,256,128]{2,1,0:T(8,128)} %copy-done) | copy-start | bytes 1966084
  25.3 15.0 %copy-start.5 = (bf16[512,512]{1,0:T(8,128)(2,1)S(1)}, bf16[512,512]{1,0:T(8,128)(2,1)}, u32[]{:S(2)}) copy-start(bf16[512,512]{1,0:T(8,128)(2,1)} %get-tuple-element.23.post_inner_ref) | copy-start | bytes 1572868
  25.3 15.0 %copy-start.6 = (bf16[512,512]{1,0:T(8,128)(2,1)S(1)}, bf16[512,512]{1,0:T(8,128)(2,1)}, u32[]{:S(2)}) copy-start(bf16[512,512]{1,0:T(8,128)(2,1)} %get-tuple-element.24.post_outer_ref) | copy-start | bytes 1572868
  25.3 15.1 %copy-start.7 = (bf16[512,512]{1,0:T(8,128)(2,1)S(1)}, bf16[512,512]{1,0:T(8,128)(2,1)}, u32[]{:S(2)}) copy-start(bf16[512,512]{1,0:T(8,128)(2,1)} %get-tuple-element.25.inner_ref) | copy-start | bytes 1572868
  25.3 15.1 %copy-start.8 = (bf16[512,512]{1,0:T(8,128)(2,1)S(1)}, bf16[512,512]{1,0:T(8,128)(2,1)}, u32[]{:S(2)}) copy-start(bf16[512,512]{1,0:T(8,128)(2,1)} %get-tuple-element.26.outer_ref) | copy-start | bytes 1572868
  25.3 15.1 %copy-start.9 = (bf16[2,512,64]{1,2,0:T(8,128)(2,1)S(1)}, bf16[2,512,64]{1,2,0:T(8,128)(2,1)}, u32[]{:S(2)}) copy-start(bf16[2,512,64]{1,2,0:T(8,128)(2,1)} %param.23) | copy-start | bytes 393220
  25.3 15.1 %copy-start.10 = (bf16[2,64,512]{2,1,0:T(8,128)(2,1)S(1)}, bf16[2,64,512]{2,1,0:T(8,128)(2,1)}, u32[]{:S(2)}) copy-start(bf16[2,64,512]{2,1,0:T(8,128)(2,1)} %up_ref.3) | copy-start | bytes 393220
  25.3 15.1 %copy-start.11 = (s32[1,32,64]{2,1,0:T(8,128)S(1)}, s32[1,32,64]{2,1,0:T(8,128)}, u32[]{:S(2)}) copy-start(s32[1,32,64]{2,1,0:T(8,128)} %param.16) | copy-start | bytes 24580
  62.7 13.9 %copy-start.2 = (bf16[2048,512]{1,0:T(8,128)(2,1)S(1)}, bf16[2048,512]{1,0:T(8,128)(2,1)}, u32[]{:S(2)}) copy-start(bf16[2048,512]{1,0:T(8,128)(2,1)} %get-tuple-element.28.x_ref) | copy-start | bytes 6291460
  62.7 13.9 %copy-start.3 = (bf16[512,512]{1,0:T(8,128)(2,1)S(1)}, bf16[512,512]{1,0:T(8,128)(2,1)}, u32[]{:S(2)}) copy-start(bf16[512,512]{1,0:T(8,128)(2,1)} %get-tuple-element.29.post_inner_ref) | copy-start | bytes 1572868
  62.7 13.9 %copy-start.4 = (bf16[512,512]{1,0:T(8,128)(2,1)S(1)}, bf16[512,512]{1,0:T(8,128)(2,1)}, u32[]{:S(2)}) copy-start(bf16[512,512]{1,0:T(8,128)(2,1)} %get-tuple-element.30.post_outer_ref) | copy-start | bytes 1572868

commit v3 on v2

--- a/solution.py
+++ b/solution.py
@@ -142,7 +142,8 @@
     down_hbm,
     post_inner_hbm,
     post_outer_hbm,
-    out_hbm,
+    out_low_hbm,
+    out_high_hbm,
     payload_ref,
     *rest,
 ):
@@ -183,7 +184,8 @@
     loads = Fetch(load_sems, [(w.at[n], split_ref.at[k]) for k, (w, n) in enumerate(split)])
     inner_half, outer_half, down_half = half_weight(inner_ref), half_weight(outer_ref), half_weight(down_ref)
     halves = [slice(0, rows_half), slice(rows_half, 2 * rows_half)]
-    stores = [pltpu.make_async_copy(out_ref.at[h], out_hbm.at[h], out_sems.at[k]) for k, h in enumerate(halves)]
+    outs = [out_low_hbm, out_high_hbm]
+    stores = [pltpu.make_async_copy(out_ref.at[h], outs[k], out_sems.at[k]) for k, h in enumerate(halves)]
     for k, c in enumerate(row_chunks(x_ref)):
         if c.start == rows_half:
             stores[0].start()
@@ -244,7 +246,8 @@
     layer,
     incoming_ref,
     return_low_ref,
-    x_hbm,
+    x_low_ref,
+    x_high_hbm,
     up_ref,
     post_inner_ref,
     post_outer_ref,
@@ -254,7 +257,7 @@
     outer_ref,
     out_hbm,
     payload_ref,
-    x_ref,
+    x_high_ref,
     out_ref,
     message_ref,
     table_ref,
@@ -262,21 +265,22 @@
     sems,
     out_sems,
 ):
-    rows_half = x_ref.shape[0] // 2
+    rows_half = x_low_ref.shape[0]
     halves = [slice(0, rows_half), slice(rows_half, 2 * rows_half)]
-    fetch = Fetch(sems, [(x_hbm.at[h], x_ref.at[h]) for h in halves])
+    fetch = Fetch(sems, [(x_high_hbm, x_high_ref)])
     stores = [pltpu.make_async_copy(out_ref.at[h], out_hbm.at[h], out_sems.at[k]) for k, h in enumerate(halves)]
     gather_messages(incoming_ref, return_low_ref, message_ref)
     up_half = half_weight(up_ref.at[layer])
     post_inner_half, post_outer_half = half_weight(post_inner_ref), half_weight(post_outer_ref)
     inner_half, outer_half = half_weight(inner_ref), half_weight(outer_ref)
     down_half = half_weight(down_ref.at[layer + 1])
-    fetch.wait(0)
-    for k, c in enumerate(row_chunks(x_ref)):
+    for k, c in enumerate(row_chunks(out_ref)):
         if c.start == rows_half:
             stores[0].start()
-            fetch.wait(1)
-        joined = join_rows(x_ref[c, :], message_ref[:, k * LANES : (k + 1) * LANES], up_half)
+            fetch.wait()
+        half, base = divmod(c.start, rows_half)
+        x = (x_low_ref, x_high_ref)[half][base : base + PAIR, :]
+        joined = join_rows(x, message_ref[:, k * LANES : (k + 1) * LANES], up_half)
         state = residual_rows(joined, post_inner_half, post_outer_half)
         rows = residual_rows(state, inner_half, outer_half)
         out_ref[c, :] = rows
@@ -573,17 +577,19 @@
 
     weight_shape = shape_of((depth, depth), bf16)
     splits = 2 * layers + 2 * (layers - 1)
-    inner, payload, *weights = run(
+    half_shape = shape_of((rows // 2, depth), bf16)
+    inner_low, inner_high, payload, *weights = run(
         functools.partial(first_kernel, layers),
         "first",
         [IN_HBM] * 7,
-        [(IN_HBM, row_shape), (IN_VMEM, payload_shape)] + [(IN_HBM, weight_shape)] * splits,
+        [(IN_HBM, half_shape)] * 2 + [(IN_VMEM, payload_shape)] + [(IN_HBM, weight_shape)] * splits,
         [row_scratch, like(send), of_layer(pre_inner), of_layer(pre_outer), of_layer(down_t), row_scratch, wide_scratch]
         + [packed_scratch, pltpu.VMEM((splits, depth, depth), bf16)]
         + [pltpu.SemaphoreType.DMA((n,)) for n in (6, 2, splits, splits)],
         (bond_states, send, pre_inner, pre_outer, down_t, post_inner, post_outer),
         mib=60,
     )
+    inner = (inner_low, inner_high)
     post_inners, post_outers = weights[:layers], weights[layers : 2 * layers]
     pre_inners = [None] + weights[2 * layers : 3 * layers - 1]
     pre_outers = [None] + weights[3 * layers - 1 :]
@@ -620,18 +626,19 @@
             (arrived, source, basis),
         )
         incoming = exchange(slot_sums, SLOT_ROWS)
-        head = (incoming, return_low, inner, up_proj, post_inners[layer], post_outers[layer])
+        head = (incoming, return_low, *inner, up_proj, post_inners[layer], post_outers[layer])
         if layer + 1 < layers:
-            inner, payload = run(
+            rows_out, payload = run(
                 functools.partial(middle_kernel, layer),
                 "middle",
-                [IN_VMEM] * 2 + [IN_HBM] + [IN_VMEM] * 7,
+                [IN_VMEM] * 3 + [IN_HBM] + [IN_VMEM] * 7,
                 [(IN_HBM, row_shape), (IN_VMEM, payload_shape)],
-                [row_scratch, row_scratch, wide_scratch, wide_scratch, packed_scratch]
-                + [pltpu.SemaphoreType.DMA((2,)), pltpu.SemaphoreType.DMA((2,))],
+                [like(half_shape), row_scratch, wide_scratch, wide_scratch, packed_scratch]
+                + [pltpu.SemaphoreType.DMA((1,)), pltpu.SemaphoreType.DMA((2,))],
                 head + (send, down_t, pre_inners[layer + 1], pre_outers[layer + 1]),
                 mib=49,
             )
+            inner = (rows_out,)
         else:
             (out,) = run(
                 functools.partial(last_kernel, layer),

time: 82.1 us -> 81 us (0.987)
  Pallas kernels: 33 us -> 31.9 us
    pallas_call x6, Pallas kernels: 33 us -> 31.9 us  [run(): pl.pallas_call(kernel, in_specs=in_specs, out_specs=list(out_specs), out_...]
    unnamed x34 -> x36, local copies, waits for them, and re-layouts: 4.1 us -> 4.15 us
where the time goes in v3:
time: 81 us; the launch traced here: 80.7 us
  blocking collectives  32.7 us (40%)
  Pallas kernels  31.9 us (39%)
  starting transfers between devices  7.43 us (9%)
  local copies, waits for them, and re-layouts  4.15 us (5%)
  waiting for transfers between devices  3.45 us (4%)
  between operations  1.02 us (1%)
    all_to_all x3, blocking collectives, exchange(): got = lax.all_to_all(values, axes, split_axis=0, concat_axis=0, tiled=True)  32.7 us
    pallas_call x6, Pallas kernels, run(): pl.pallas_call(kernel, in_specs=in_specs, out_specs=list(out_specs), out_...  31.9 us
    all_to_all x1, starting transfers between devices, exchange(): got = lax.all_to_all(values, axes, split_axis=0, concat_axis=0, tiled=True)  7.43 us
    unnamed x36, local copies, waits for them, and re-layouts  4.15 us
    all_to_all x1, waiting for transfers between devices, exchange(): got = lax.all_to_all(values, axes, split_axis=0, concat_axis=0, tiled=True)  3.45 us
  transfers between devices with their start and end apart: 1, of which 1 were waited for; matrix products, arithmetic and copies ran while one was open for 0% of the time, Pallas kernels for 3%

profile of v3, /device:TPU:0, one launch (start us, length us, event | category | flops | bytes accessed | tf_op | source)
XLA Modules:
  0.0 80.7 jit_solution(9871655839941538177)
XLA Ops:
  0.0 0.0 copy-start.15
  0.0 0.0 copy-start.16
  0.0 7.2 %first.1 = (bf16[1024,512]{1,0:T(8,128)(2,1)}, bf16[1024,512]{1,0:T(8,128)(2,1)}, bf16[1024,128]{1,0:T(8,128)(2,1)}, bf16[512,512]{1,0:T(8,128)(2,1)}, bf16[512,...) custom-call(bf16[2048,512]{1,0:T(8,128)(2,1)} %x_hbm.1, ...), custom_call_target="tpu_custom_call" | custom-call | flops 1000000000 | bytes 8000000 | tf_op jit(solution)/shard_map/first/pallas_call | solution.py:514
  7.2 7.4 %all-to-all-start = ((bf16[32,32,128]{2,1,0:T(8,128)(2,1)}), bf16[32,32,128]{2,1,0:T(8,128)(2,1)}, u32[]{:S(2)}, u32[]{:S(2)}) async-start(bf16[32,32,128]{2,1,0:T(8,128)(2,1)} %bitcast.22), calls=%async_computation | async-start | bytes 524288 | tf_op jit(solution)/shard_map/all_to_all | solution.py:575
  15.3 0.0 copy-done.15
  15.3 0.0 copy-done.16
  15.3 0.0 copy-start.13
  15.3 1.6 %copy-done.13 = bf16[64,32,512]{2,1,0:T(8,128)(2,1)S(1)} copy-done((bf16[64,32,512]{2,1,0:T(8,128)(2,1)S(1)}, bf16[64,32,512]{2,1,0:T(8,128)(2,1)}, u32[]{:S(2)}) %copy-start.13) | copy-done | bytes 2097176
  16.9 0.0 copy-start.14
  16.9 0.9 %copy-done.14 = bf16[2,1024,64]{1,2,0:T(8,128)(2,1)S(1)} copy-done((bf16[2,1024,64]{1,2,0:T(8,128)(2,1)S(1)}, bf16[2,1024,64]{1,2,0:T(8,128)(2,1)}, u32[]{:S(2)}) %copy-start.14) | copy-done | bytes 262168
  17.9 0.0 copy-start.17
  17.9 0.7 copy-done.17
  18.5 2.4 %prepare.1 = (bf16[9,512,256]{2,1,0:T(8,128)(2,1)S(1)}, s32[9,256,128]{2,1,0:T(8,128)S(1)}, s32[5,256,128]{2,1,0:T(8,128)S(1)}) custom-call(s32[1]{0:T(128)S(6)} %copy.15.counts_ref, s32[1,2048]{1,0:T(1,128)S(1)} %copy-done.15, s32[1,2048]{1,0:T(1,128)S(1)} %copy-done.16, s32[1,1024]{1,0:T(1,128)S(1)} %copy-done.17, bf16[64,32,512]{2,1,0:T(8,128)(2,1)S(1)} %copy-done.13, ...), custom_call_target="tpu_custom_call" | custom-call | flops 4000000000 | bytes 8000000 | tf_op jit(solution)/shard_map/prepare/pallas_call | solution.py:514
  20.9 0.0 copy-start
  21.0 0.9 %copy-done = s32[5,256,128]{2,1,0:T(8,128)} copy-done((s32[5,256,128]{2,1,0:T(8,128)}, s32[5,256,128]{2,1,0:T(8,128)S(1)}, u32[]{:S(2)}) %copy-start) | copy-done | bytes 655384
  21.8 3.5 %all-to-all-done = bf16[32,32,128]{2,1,0:T(8,128)(2,1)} async-done(((bf16[32,32,128]{2,1,0:T(8,128)(2,1)}), bf16[32,32,128]{2,1,0:T(8,128)(2,1)}, u32[]{:S(2)}, u32[]{:S(2)}) %all-to-all-start) | async-done | bytes 262176 | tf_op jit(solution)/shard_map/all_to_all | solution.py:575
  25.3 0.0 copy-start.1
  25.3 0.0 copy-start.3
  25.3 0.0 copy-start.6
  25.3 0.0 copy-start.7
  25.3 0.0 copy-start.8
  25.3 0.0 copy-start.9
  25.3 0.0 copy-start.10
  25.3 0.0 copy-start.11
  25.3 0.0 copy-start.12
  25.3 5.1 %owner.2 = bf16[256,256]{1,0:T(8,128)(2,1)S(1)} custom-call(bf16[1024,128]{1,0:T(8,128)(2,1)} %bitcast.3.arrived_ref, s32[9,256,128]{2,1,0:T(8,128)S(1)} %get-tuple-element.20.source_ref, bf16[9,512,256]{2,1,0:T(8,128)(2,1)S(1)} %get-tuple-element.21.basis_ref), custom_call_target="tpu_custom_call" | custom-call | flops 1000000000 | bytes 8000000 | tf_op jit(solution)/shard_map/owner/pallas_call | solution.py:514
  30.4 9.9 %all_to_all.20 = bf16[32,8,256]{2,1,0:T(8,128)(2,1)S(1)} all-to-all(bf16[32,8,256]{2,1,0:T(8,128)(2,1)S(1)} %bitcast.17), channel_id=1, replica_groups=mesh['bond'=4,'atom'=8] {'bond','atom'}, dimensions={0} | all-to-all | bytes 262144 | tf_op jit(solution)/shard_map/all_to_all | solution.py:575
  40.3 0.0 copy-done.1
  40.3 0.0 copy-done.3
  40.3 0.0 copy-done.6
  40.3 0.0 copy-done.7
  40.3 0.0 copy-done.8
  40.4 0.0 copy-done.9
  40.4 0.0 copy-done.10
  40.4 0.0 copy-done.11
  40.4 0.0 copy-done.12
  40.4 8.3 %middle.1 = (bf16[2048,512]{1,0:T(8,128)(2,1)}, bf16[1024,128]{1,0:T(8,128)(2,1)S(1)}) custom-call(bf16[256,256]{1,0:T(8,128)(2,1)S(1)} %bitcast.14, s32[5,256,128]{2,1,0:T(8,128)S(1)} %copy-done.1, bf16[1024,512]{1,0:T(8,128)(2,1)S(1)} %copy-done.3, bf16[1024,512]{1,0:T(8,128)(2,1)} %get-tuple-element.24.x_high_hbm, bf16[2,64,512]{2,1,0:T(8,128)(2,1)S(1)} %copy-done.11, ...), custom_call_target="tpu_custom_call" | custom-call | flops 1000000000 | bytes 8000000 | tf_op jit(solution)/shard_map/middle/pallas_call | solution.py:514
  48.7 12.9 %all_to_all.21 = bf16[32,32,128]{2,1,0:T(8,128)(2,1)S(1)} all-to-all(bf16[32,32,128]{2,1,0:T(8,128)(2,1)S(1)} %bitcast.18), channel_id=1, replica_groups=mesh['bond'=4,'atom'=8] {'bond','atom'}, dimensions={0} | all-to-all | bytes 524288 | tf_op jit(solution)/shard_map/all_to_all | solution.py:575
  61.6 0.0 copy-start.2
  61.6 0.0 copy-start.4
  61.7 0.0 copy-start.5
  61.7 3.9 %owner.3 = bf16[256,256]{1,0:T(8,128)(2,1)S(1)} custom-call(bf16[1024,128]{1,0:T(8,128)(2,1)S(1)} %bitcast.11, s32[9,256,128]{2,1,0:T(8,128)S(1)} %get-tuple-element.20.source_ref, bf16[9,512,256]{2,1,0:T(8,128)(2,1)S(1)} %get-tuple-element.21.basis_ref), custom_call_target="tpu_custom_call" | custom-call | flops 1000000000 | bytes 8000000 | tf_op jit(solution)/shard_map/owner/pallas_call | solution.py:514
  65.6 9.9 %all_to_all.22 = bf16[32,8,256]{2,1,0:T(8,128)(2,1)S(1)} all-to-all(bf16[32,8,256]{2,1,0:T(8,128)(2,1)S(1)} %bitcast.16), channel_id=1, replica_groups=mesh['bond'=4,'atom'=8] {'bond','atom'}, dimensions={0} | all-to-all | bytes 262144 | tf_op jit(solution)/shard_map/all_to_all | solution.py:575
  75.5 0.0 copy-done.2
  75.5 0.0 copy-done.4
  75.5 0.0 copy-done.5
  75.5 5.0 %last.1 = bf16[2048,512]{1,0:T(8,128)(2,1)} custom-call(bf16[256,256]{1,0:T(8,128)(2,1)S(1)} %bitcast.15, s32[5,256,128]{2,1,0:T(8,128)S(1)} %copy-done.1, bf16[2048,512]{1,0:T(8,128)(2,1)S(1)} %copy-done.2, bf16[2,64,512]{2,1,0:T(8,128)(2,1)S(1)} %copy-done.11, bf16[512,512]{1,0:T(8,128)(2,1)S(1)} %copy-done.4, bf16[512,512]{1,0:T(8,128)(2,1)S(1)} %copy-done.5), custom_call_target="tpu_custom_call" | custom-call | flops 1000000000 | bytes 8000000 | tf_op jit(solution)/shard_map/last/pallas_call | solution.py:514
Async XLA Ops:
  0.0 15.3 %copy-start.15 = (s32[1,2048]{1,0:T(1,128)S(1)}, s32[1,2048]{1,0:T(1,128)}, u32[]{:S(2)}) copy-start(s32[1,2048]{1,0:T(1,128)} %source_ref.1) | copy-start | bytes 24580
  0.0 15.3 %copy-start.16 = (s32[1,2048]{1,0:T(1,128)S(1)}, s32[1,2048]{1,0:T(1,128)}, u32[]{:S(2)}) copy-start(s32[1,2048]{1,0:T(1,128)} %target_ref.1) | copy-start | bytes 24580
  7.2 18.1 %all-to-all-start = ((bf16[32,32,128]{2,1,0:T(8,128)(2,1)}), bf16[32,32,128]{2,1,0:T(8,128)(2,1)}, u32[]{:S(2)}, u32[]{:S(2)}) async-start(bf16[32,32,128]{2,1,0:T(8,128)(2,1)} %bitcast.22), calls=%async_computation | async-start | bytes 524288 | tf_op jit(solution)/shard_map/all_to_all | solution.py:575
  15.3 1.6 %copy-start.13 = (bf16[64,32,512]{2,1,0:T(8,128)(2,1)S(1)}, bf16[64,32,512]{2,1,0:T(8,128)(2,1)}, u32[]{:S(2)}) copy-start(bf16[64,32,512]{2,1,0:T(8,128)(2,1)} %basis_hbm.1) | copy-start | bytes 6291460
  16.9 0.9 %copy-start.14 = (bf16[2,1024,64]{1,2,0:T(8,128)(2,1)S(1)}, bf16[2,1024,64]{1,2,0:T(8,128)(2,1)}, u32[]{:S(2)}) copy-start(bf16[2,1024,64]{1,2,0:T(8,128)(2,1)} %param.24) | copy-start | bytes 786436
  17.9 0.7 copy-start.17
  20.9 0.9 %copy-start = (s32[5,256,128]{2,1,0:T(8,128)}, s32[5,256,128]{2,1,0:T(8,128)S(1)}, u32[]{:S(2)}) copy-start(s32[5,256,128]{2,1,0:T(8,128)S(1)} %get-tuple-element.22.return_low_ref) | copy-start | bytes 1966084
  25.3 15.1 %copy-start.1 = (s32[5,256,128]{2,1,0:T(8,128)S(1)}, s32[5,256,128]{2,1,0:T(8,128)}, u32[]{:S(2)}) copy-start(s32[5,256,128]{2,1,0:T(8,128)} %copy-done) | copy-start | bytes 1966084
  25.3 15.1 %copy-start.3 = (bf16[1024,512]{1,0:T(8,128)(2,1)S(1)}, bf16[1024,512]{1,0:T(8,128)(2,1)}, u32[]{:S(2)}) copy-start(bf16[1024,512]{1,0:T(8,128)(2,1)} %get-tuple-element.23.x_low_ref) | copy-start | bytes 3145732
  25.3 15.1 %copy-start.6 = (bf16[512,512]{1,0:T(8,128)(2,1)S(1)}, bf16[512,512]{1,0:T(8,128)(2,1)}, u32[]{:S(2)}) copy-start(bf16[512,512]{1,0:T(8,128)(2,1)} %get-tuple-element.25.post_inner_ref) | copy-start | bytes 1572868
  25.3 15.1 %copy-start.7 = (bf16[512,512]{1,0:T(8,128)(2,1)S(1)}, bf16[512,512]{1,0:T(8,128)(2,1)}, u32[]{:S(2)}) copy-start(bf16[512,512]{1,0:T(8,128)(2,1)} %get-tuple-element.26.post_outer_ref) | copy-start | bytes 1572868
  25.3 15.1 %copy-start.8 = (bf16[512,512]{1,0:T(8,128)(2,1)S(1)}, bf16[512,512]{1,0:T(8,128)(2,1)}, u32[]{:S(2)}) copy-start(bf16[512,512]{1,0:T(8,128)(2,1)} %get-tuple-element.27.inner_ref) | copy-start | bytes 1572868
  25.3 15.1 %copy-start.9 = (bf16[512,512]{1,0:T(8,128)(2,1)S(1)}, bf16[512,512]{1,0:T(8,128)(2,1)}, u32[]{:S(2)}) copy-start(bf16[512,512]{1,0:T(8,128)(2,1)} %get-tuple-element.28.outer_ref) | copy-start | bytes 1572868
  25.3 15.1 %copy-start.10 = (bf16[2,512,64]{1,2,0:T(8,128)(2,1)S(1)}, bf16[2,512,64]{1,2,0:T(8,128)(2,1)}, u32[]{:S(2)}) copy-start(bf16[2,512,64]{1,2,0:T(8,128)(2,1)} %param.23) | copy-start | bytes 393220
  25.3 15.1 %copy-start.11 = (bf16[2,64,512]{2,1,0:T(8,128)(2,1)S(1)}, bf16[2,64,512]{2,1,0:T(8,128)(2,1)}, u32[]{:S(2)}) copy-start(bf16[2,64,512]{2,1,0:T(8,128)(2,1)} %up_ref.3) | copy-start | bytes 393220
  25.3 15.1 %copy-start.12 = (s32[1,32,64]{2,1,0:T(8,128)S(1)}, s32[1,32,64]{2,1,0:T(8,128)}, u32[]{:S(2)}) copy-start(s32[1,32,64]{2,1,0:T(8,128)} %param.16) | copy-start | bytes 24580
  61.6 13.9 %copy-start.2 = (bf16[2048,512]{1,0:T(8,128)(2,1)S(1)}, bf16[2048,512]{1,0:T(8,128)(2,1)}, u32[]{:S(2)}) copy-start(bf16[2048,512]{1,0:T(8,128)(2,1)} %get-tuple-element.30.x_ref) | copy-start | bytes 6291460
  61.6 13.9 %copy-start.4 = (bf16[512,512]{1,0:T(8,128)(2,1)S(1)}, bf16[512,512]{1,0:T(8,128)(2,1)}, u32[]{:S(2)}) copy-start(bf16[512,512]{1,0:T(8,128)(2,1)} %get-tuple-element.31.post_inner_ref) | copy-start | bytes 1572868
  61.7 13.9 %copy-start.5 = (bf16[512,512]{1,0:T(8,128)(2,1)S(1)}, bf16[512,512]{1,0:T(8,128)(2,1)}, u32[]{:S(2)}) copy-start(bf16[512,512]{1,0:T(8,128)(2,1)} %get-tuple-element.32.post_outer_ref) | copy-start | bytes 1572868

commit v4 on v3

--- a/solution.py
+++ b/solution.py
@@ -148,7 +148,7 @@
     *rest,
 ):
     layer = 0
-    split = [(w, n) for w in (post_inner_hbm, post_outer_hbm) for n in range(layers)]
+    split = [(w, n) for w in (post_inner_hbm, post_outer_hbm) for n in range(layers - 1)]
     split += [(w, n) for w in (inner_hbm, outer_hbm) for n in range(1, layers)]
     split_out = rest[: len(split)]
     (
@@ -307,7 +307,7 @@
 ):
     gather_messages(incoming_ref, return_low_ref, message_ref)
     up_half = half_weight(up_ref.at[layer])
-    post_inner_half, post_outer_half = half_weight(post_inner_ref), half_weight(post_outer_ref)
+    post_inner_half, post_outer_half = half_weight(post_inner_ref.at[layer]), half_weight(post_outer_ref.at[layer])
     chunks = row_chunks(x_ref)
     stores = []
     count = len(chunks)
@@ -576,7 +576,7 @@
         return got.reshape(peers * per_peer, values.shape[2])
 
     weight_shape = shape_of((depth, depth), bf16)
-    splits = 2 * layers + 2 * (layers - 1)
+    splits = 4 * (layers - 1)
     half_shape = shape_of((rows // 2, depth), bf16)
     inner_low, inner_high, payload, *weights = run(
         functools.partial(first_kernel, layers),
@@ -590,9 +590,9 @@
         mib=60,
     )
     inner = (inner_low, inner_high)
-    post_inners, post_outers = weights[:layers], weights[layers : 2 * layers]
-    pre_inners = [None] + weights[2 * layers : 3 * layers - 1]
-    pre_outers = [None] + weights[3 * layers - 1 :]
+    later = layers - 1
+    post_inners, post_outers = weights[:later] + [post_inner], weights[later : 2 * later] + [post_outer]
+    pre_inners, pre_outers = [None] + weights[2 * later : 3 * later], [None] + weights[3 * later :]
 
     parts = cap_back // SLOT_ROWS
     basis, source, return_low = run(

time: 81 us -> 81 us (level)
  no operation moved by 1% of the time
where the time goes in v4:
time: 81 us; the launch traced here: 80.6 us
  blocking collectives  32.7 us (40%)
  Pallas kernels  31.9 us (39%)
  starting transfers between devices  7.43 us (9%)
  local copies, waits for them, and re-layouts  4.15 us (5%)
  waiting for transfers between devices  3.45 us (4%)
  between operations  1.02 us (1%)
    all_to_all x3, blocking collectives, exchange(): got = lax.all_to_all(values, axes, split_axis=0, concat_axis=0, tiled=True)  32.7 us
    pallas_call x6, Pallas kernels, run(): pl.pallas_call(kernel, in_specs=in_specs, out_specs=list(out_specs), out_...  31.9 us
    all_to_all x1, starting transfers between devices, exchange(): got = lax.all_to_all(values, axes, split_axis=0, concat_axis=0, tiled=True)  7.43 us
    unnamed x36, local copies, waits for them, and re-layouts  4.15 us
    all_to_all x1, waiting for transfers between devices, exchange(): got = lax.all_to_all(values, axes, split_axis=0, concat_axis=0, tiled=True)  3.45 us
  transfers between devices with their start and end apart: 1, of which 1 were waited for; matrix products, arithmetic and copies ran while one was open for 0% of the time, Pallas kernels for 3%

profile of v4, /device:TPU:0, one launch (start us, length us, event | category | flops | bytes accessed | tf_op | source)
XLA Modules:
  0.0 80.6 jit_solution(10472569857785417994)
XLA Ops:
  0.0 0.0 copy-start.15
  0.0 0.0 copy-start.16
  0.0 7.1 %first.1 = (bf16[1024,512]{1,0:T(8,128)(2,1)}, bf16[1024,512]{1,0:T(8,128)(2,1)}, bf16[1024,128]{1,0:T(8,128)(2,1)}, bf16[512,512]{1,0:T(8,128)(2,1)}, bf16[512,...) custom-call(bf16[2048,512]{1,0:T(8,128)(2,1)} %x_hbm.1, s32[32,64]{1,0:T(8,128)} %bitcast.19, ...), custom_call_target="tpu_custom_call" | custom-call | flops 1000000000 | bytes 8000000 | tf_op jit(solution)/shard_map/first/pallas_call | solution.py:514
  7.1 7.4 %all-to-all-start = ((bf16[32,32,128]{2,1,0:T(8,128)(2,1)}), bf16[32,32,128]{2,1,0:T(8,128)(2,1)}, u32[]{:S(2)}, u32[]{:S(2)}) async-start(bf16[32,32,128]{2,1,0:T(8,128)(2,1)} %bitcast.22), calls=%async_computation | async-start | bytes 524288 | tf_op jit(solution)/shard_map/all_to_all | solution.py:575
  15.2 0.0 copy-done.15
  15.2 0.0 copy-done.16
  15.3 0.0 copy-start.13
  15.3 1.6 %copy-done.13 = bf16[64,32,512]{2,1,0:T(8,128)(2,1)S(1)} copy-done((bf16[64,32,512]{2,1,0:T(8,128)(2,1)S(1)}, bf16[64,32,512]{2,1,0:T(8,128)(2,1)}, u32[]{:S(2)}) %copy-start.13) | copy-done | bytes 2097176
  16.9 0.0 copy-start.14
  16.9 0.9 %copy-done.14 = bf16[2,1024,64]{1,2,0:T(8,128)(2,1)S(1)} copy-done((bf16[2,1024,64]{1,2,0:T(8,128)(2,1)S(1)}, bf16[2,1024,64]{1,2,0:T(8,128)(2,1)}, u32[]{:S(2)}) %copy-start.14) | copy-done | bytes 262168
  17.8 0.0 copy-start.17
  17.8 0.7 copy-done.17
  18.5 2.4 %prepare.1 = (bf16[9,512,256]{2,1,0:T(8,128)(2,1)S(1)}, s32[9,256,128]{2,1,0:T(8,128)S(1)}, s32[5,256,128]{2,1,0:T(8,128)S(1)}) custom-call(s32[1]{0:T(128)S(6)} %copy.15.counts_ref, s32[1,2048]{1,0:T(1,128)S(1)} %copy-done.15, s32[1,2048]{1,0:T(1,128)S(1)} %copy-done.16, s32[1,1024]{1,0:T(1,128)S(1)} %copy-done.17, bf16[64,32,512]{2,1,0:T(8,128)(2,1)S(1)} %copy-done.13, ...), custom_call_target="tpu_custom_call" | custom-call | flops 4000000000 | bytes 8000000 | tf_op jit(solution)/shard_map/prepare/pallas_call | solution.py:514
  20.9 0.0 copy-start.2
  20.9 0.9 %copy-done.2 = s32[5,256,128]{2,1,0:T(8,128)} copy-done((s32[5,256,128]{2,1,0:T(8,128)}, s32[5,256,128]{2,1,0:T(8,128)S(1)}, u32[]{:S(2)}) %copy-start.2) | copy-done | bytes 655384
  21.8 3.5 %all-to-all-done = bf16[32,32,128]{2,1,0:T(8,128)(2,1)} async-done(((bf16[32,32,128]{2,1,0:T(8,128)(2,1)}), bf16[32,32,128]{2,1,0:T(8,128)(2,1)}, u32[]{:S(2)}, u32[]{:S(2)}) %all-to-all-start) | async-done | bytes 262176 | tf_op jit(solution)/shard_map/all_to_all | solution.py:575
  25.2 0.0 copy-start.3
  25.2 0.0 copy-start.5
  25.2 0.0 copy-start.6
  25.2 0.0 copy-start.7
  25.2 0.0 copy-start.8
  25.2 0.0 copy-start.9
  25.2 0.0 copy-start.10
  25.3 0.0 copy-start.11
  25.3 0.0 copy-start.12
  25.3 5.1 %owner.2 = bf16[256,256]{1,0:T(8,128)(2,1)S(1)} custom-call(bf16[1024,128]{1,0:T(8,128)(2,1)} %bitcast.3.arrived_ref, s32[9,256,128]{2,1,0:T(8,128)S(1)} %get-tuple-element.18.source_ref, bf16[9,512,256]{2,1,0:T(8,128)(2,1)S(1)} %get-tuple-element.19.basis_ref), custom_call_target="tpu_custom_call" | custom-call | flops 1000000000 | bytes 8000000 | tf_op jit(solution)/shard_map/owner/pallas_call | solution.py:514
  30.4 9.9 %all_to_all.20 = bf16[32,8,256]{2,1,0:T(8,128)(2,1)S(1)} all-to-all(bf16[32,8,256]{2,1,0:T(8,128)(2,1)S(1)} %bitcast.17), channel_id=1, replica_groups=mesh['bond'=4,'atom'=8] {'bond','atom'}, dimensions={0} | all-to-all | bytes 262144 | tf_op jit(solution)/shard_map/all_to_all | solution.py:575
  40.3 0.0 copy-done.3
  40.3 0.0 copy-done.5
  40.3 0.0 copy-done.6
  40.3 0.0 copy-done.7
  40.3 0.0 copy-done.8
  40.3 0.0 copy-done.9
  40.3 0.0 copy-done.10
  40.3 0.0 copy-done.11
  40.3 0.0 copy-done.12
  40.3 8.3 %middle.1 = (bf16[2048,512]{1,0:T(8,128)(2,1)}, bf16[1024,128]{1,0:T(8,128)(2,1)S(1)}) custom-call(bf16[256,256]{1,0:T(8,128)(2,1)S(1)} %bitcast.15, s32[5,256,128]{2,1,0:T(8,128)S(1)} %copy-done.3, bf16[1024,512]{1,0:T(8,128)(2,1)S(1)} %copy-done.5, bf16[1024,512]{1,0:T(8,128)(2,1)} %get-tuple-element.22.x_high_hbm, bf16[2,64,512]{2,1,0:T(8,128)(2,1)S(1)} %copy-done.6, ...), custom_call_target="tpu_custom_call" | custom-call | flops 1000000000 | bytes 8000000 | tf_op jit(solution)/shard_map/middle/pallas_call | solution.py:514
  48.7 12.9 %all_to_all.21 = bf16[32,32,128]{2,1,0:T(8,128)(2,1)S(1)} all-to-all(bf16[32,32,128]{2,1,0:T(8,128)(2,1)S(1)} %bitcast.18), channel_id=1, replica_groups=mesh['bond'=4,'atom'=8] {'bond','atom'}, dimensions={0} | all-to-all | bytes 524288 | tf_op jit(solution)/shard_map/all_to_all | solution.py:575
  61.6 0.0 copy-start
  61.6 0.0 copy-start.1
  61.6 0.0 copy-start.4
  61.6 3.9 %owner.3 = bf16[256,256]{1,0:T(8,128)(2,1)S(1)} custom-call(bf16[1024,128]{1,0:T(8,128)(2,1)S(1)} %bitcast.11, s32[9,256,128]{2,1,0:T(8,128)S(1)} %get-tuple-element.18.source_ref, bf16[9,512,256]{2,1,0:T(8,128)(2,1)S(1)} %get-tuple-element.19.basis_ref), custom_call_target="tpu_custom_call" | custom-call | flops 1000000000 | bytes 8000000 | tf_op jit(solution)/shard_map/owner/pallas_call | solution.py:514
  65.5 9.9 %all_to_all.22 = bf16[32,8,256]{2,1,0:T(8,128)(2,1)S(1)} all-to-all(bf16[32,8,256]{2,1,0:T(8,128)(2,1)S(1)} %bitcast.16), channel_id=1, replica_groups=mesh['bond'=4,'atom'=8] {'bond','atom'}, dimensions={0} | all-to-all | bytes 262144 | tf_op jit(solution)/shard_map/all_to_all | solution.py:575
  75.4 0.0 copy-done
  75.4 0.0 copy-done.1
  75.4 0.0 copy-done.4
  75.5 5.0 %last.1 = bf16[2048,512]{1,0:T(8,128)(2,1)} custom-call(bf16[256,256]{1,0:T(8,128)(2,1)S(1)} %bitcast.12, s32[5,256,128]{2,1,0:T(8,128)S(1)} %copy-done.3, bf16[2048,512]{1,0:T(8,128)(2,1)S(1)} %copy-done.4, bf16[2,64,512]{2,1,0:T(8,128)(2,1)S(1)} %copy-done.6, bf16[2,512,512]{2,1,0:T(8,128)(2,1)S(1)} %copy-done, bf16[2,512,512]{2,1,0:T(8,128)(2,1)S(1)} %copy-done.1), custom_call_target="tpu_custom_call" | custom-call | flops 1000000000 | bytes 8000000 | tf_op jit(solution)/shard_map/last/pallas_call | solution.py:514
Async XLA Ops:
  0.0 15.2 %copy-start.15 = (s32[1,2048]{1,0:T(1,128)S(1)}, s32[1,2048]{1,0:T(1,128)}, u32[]{:S(2)}) copy-start(s32[1,2048]{1,0:T(1,128)} %source_ref.1) | copy-start | bytes 24580
  0.0 15.2 %copy-start.16 = (s32[1,2048]{1,0:T(1,128)S(1)}, s32[1,2048]{1,0:T(1,128)}, u32[]{:S(2)}) copy-start(s32[1,2048]{1,0:T(1,128)} %target_ref.1) | copy-start | bytes 24580
  7.1 18.1 %all-to-all-start = ((bf16[32,32,128]{2,1,0:T(8,128)(2,1)}), bf16[32,32,128]{2,1,0:T(8,128)(2,1)}, u32[]{:S(2)}, u32[]{:S(2)}) async-start(bf16[32,32,128]{2,1,0:T(8,128)(2,1)} %bitcast.22), calls=%async_computation | async-start | bytes 524288 | tf_op jit(solution)/shard_map/all_to_all | solution.py:575
  15.3 1.6 %copy-start.13 = (bf16[64,32,512]{2,1,0:T(8,128)(2,1)S(1)}, bf16[64,32,512]{2,1,0:T(8,128)(2,1)}, u32[]{:S(2)}) copy-start(bf16[64,32,512]{2,1,0:T(8,128)(2,1)} %basis_hbm.1) | copy-start | bytes 6291460
  16.9 0.9 %copy-start.14 = (bf16[2,1024,64]{1,2,0:T(8,128)(2,1)S(1)}, bf16[2,1024,64]{1,2,0:T(8,128)(2,1)}, u32[]{:S(2)}) copy-start(bf16[2,1024,64]{1,2,0:T(8,128)(2,1)} %param.24) | copy-start | bytes 786436
  17.8 0.7 copy-start.17
  20.9 0.9 %copy-start.2 = (s32[5,256,128]{2,1,0:T(8,128)}, s32[5,256,128]{2,1,0:T(8,128)S(1)}, u32[]{:S(2)}) copy-start(s32[5,256,128]{2,1,0:T(8,128)S(1)} %get-tuple-element.20.return_low_ref) | copy-start | bytes 1966084
  25.2 15.1 %copy-start.3 = (s32[5,256,128]{2,1,0:T(8,128)S(1)}, s32[5,256,128]{2,1,0:T(8,128)}, u32[]{:S(2)}) copy-start(s32[5,256,128]{2,1,0:T(8,128)} %copy-done.2) | copy-start | bytes 1966084
  25.2 15.1 %copy-start.5 = (bf16[1024,512]{1,0:T(8,128)(2,1)S(1)}, bf16[1024,512]{1,0:T(8,128)(2,1)}, u32[]{:S(2)}) copy-start(bf16[1024,512]{1,0:T(8,128)(2,1)} %get-tuple-element.21.x_low_ref) | copy-start | bytes 3145732
  25.2 15.1 %copy-start.6 = (bf16[2,64,512]{2,1,0:T(8,128)(2,1)S(1)}, bf16[2,64,512]{2,1,0:T(8,128)(2,1)}, u32[]{:S(2)}) copy-start(bf16[2,64,512]{2,1,0:T(8,128)(2,1)} %up_ref.3) | copy-start | bytes 393220
  25.2 15.1 %copy-start.7 = (bf16[512,512]{1,0:T(8,128)(2,1)S(1)}, bf16[512,512]{1,0:T(8,128)(2,1)}, u32[]{:S(2)}) copy-start(bf16[512,512]{1,0:T(8,128)(2,1)} %get-tuple-element.23.post_inner_ref) | copy-start | bytes 1572868
  25.2 15.1 %copy-start.8 = (bf16[512,512]{1,0:T(8,128)(2,1)S(1)}, bf16[512,512]{1,0:T(8,128)(2,1)}, u32[]{:S(2)}) copy-start(bf16[512,512]{1,0:T(8,128)(2,1)} %get-tuple-element.24.post_outer_ref) | copy-start | bytes 1572868
  25.2 15.1 %copy-start.9 = (bf16[512,512]{1,0:T(8,128)(2,1)S(1)}, bf16[512,512]{1,0:T(8,128)(2,1)}, u32[]{:S(2)}) copy-start(bf16[512,512]{1,0:T(8,128)(2,1)} %get-tuple-element.25.inner_ref) | copy-start | bytes 1572868
  25.2 15.1 %copy-start.10 = (bf16[512,512]{1,0:T(8,128)(2,1)S(1)}, bf16[512,512]{1,0:T(8,128)(2,1)}, u32[]{:S(2)}) copy-start(bf16[512,512]{1,0:T(8,128)(2,1)} %get-tuple-element.26.outer_ref) | copy-start | bytes 1572868
  25.3 15.1 %copy-start.11 = (bf16[2,512,64]{1,2,0:T(8,128)(2,1)S(1)}, bf16[2,512,64]{1,2,0:T(8,128)(2,1)}, u32[]{:S(2)}) copy-start(bf16[2,512,64]{1,2,0:T(8,128)(2,1)} %param.23) | copy-start | bytes 393220
  25.3 15.1 %copy-start.12 = (s32[1,32,64]{2,1,0:T(8,128)S(1)}, s32[1,32,64]{2,1,0:T(8,128)}, u32[]{:S(2)}) copy-start(s32[1,32,64]{2,1,0:T(8,128)} %param.16) | copy-start | bytes 24580
  61.6 13.9 %copy-start = (bf16[2,512,512]{2,1,0:T(8,128)(2,1)S(1)}, bf16[2,512,512]{2,1,0:T(8,128)(2,1)}, u32[]{:S(2)}) copy-start(bf16[2,512,512]{2,1,0:T(8,128)(2,1)} %post_inner_ref.1) | copy-start | bytes 3145732
  61.6 13.9 %copy-start.1 = (bf16[2,512,512]{2,1,0:T(8,128)(2,1)S(1)}, bf16[2,512,512]{2,1,0:T(8,128)(2,1)}, u32[]{:S(2)}) copy-start(bf16[2,512,512]{2,1,0:T(8,128)(2,1)} %post_outer_ref.1) | copy-start | bytes 3145732
  61.6 13.9 %copy-start.4 = (bf16[2048,512]{1,0:T(8,128)(2,1)S(1)}, bf16[2048,512]{1,0:T(8,128)(2,1)}, u32[]{:S(2)}) copy-start(bf16[2048,512]{1,0:T(8,128)(2,1)} %get-tuple-element.28.x_ref) | copy-start | bytes 6291460

commit v5 on v4

--- a/solution.py
+++ b/solution.py
@@ -459,10 +459,18 @@
     kept_ref,
     lhs_ref,
     spread_ref,
+    *own,
 ):
+    if own:
+        fetch = Fetch(own[2], [(arrived_ref, own[0])])
+        arrived_ref = own[0]
     slabs, span, group_rows = basis_ref.shape
     groups = slabs - 1
     spread_weight(basis_ref, layer, LANES // 2, weight_ref)
+    if own:
+        for g in range(groups):
+            own[1][g] = one_hot_rows((source_ref[g] & (HIGH - 1)).astype(f32))
+        fetch.wait()
     half_blocks = BLOCKS_IN_GROUP // 2
     width = LANES // half_blocks
     sph = span // width
@@ -472,7 +480,8 @@
     own_half = (lax.broadcasted_iota(i32, shape, 0) >= LANES) == (lane(shape) >= LANES // 2)
     for g in range(groups):
         source = source_ref[g]
-        wide = mm(one_hot_rows((source & (HIGH - 1)).astype(f32)), table)
+        pick = own[1][g] if own else one_hot_rows((source & (HIGH - 1)).astype(f32))
+        wide = mm(pick, table)
         code = (source >> 8) & (HIGH - 1)
         picked = pick_group(wide, code >> 1, tables)
         turned = jnp.where((code & 1) == 1, swap_halves(picked), picked)
@@ -615,14 +624,16 @@
         (slot_sums,) = run(
             functools.partial(owner_kernel, layer),
             "owner",
-            [IN_VMEM] * 3,
+            [IN_HBM if layer == 0 else IN_VMEM] + [IN_VMEM] * 2,
             [(IN_VMEM, shape_of((slots, slot_lanes), bf16))],
             [
                 pltpu.VMEM((bilinear.shape[1] * 2, 2 * LANES), bf16),
                 pltpu.VMEM((groups, group_rows, LANES), bf16),
                 pltpu.VMEM((blocks * width // 2, bilinear.shape[1] * 2), bf16),
                 pltpu.VMEM((blocks * width, slot_lanes), bf16),
-            ],
+            ]
+            + ([like(arrived), pltpu.VMEM((groups, group_rows, HIGH), bf16)] if layer == 0 else [])
+            + ([pltpu.SemaphoreType.DMA((1,))] if layer == 0 else []),
             (arrived, source, basis),
         )
         incoming = exchange(slot_sums, SLOT_ROWS)

time: 81 us -> 80.9 us (level)
  no operation moved by 1% of the time
where the time goes in v5:
time: 80.9 us; the launch traced here: 80.5 us
  blocking collectives  32.7 us (40%)
  Pallas kernels  31.8 us (39%)
  starting transfers between devices  7.43 us (9%)
  local copies, waits for them, and re-layouts  4.15 us (5%)
  waiting for transfers between devices  3.45 us (4%)
  between operations  1.02 us (1%)
    all_to_all x3, blocking collectives, exchange(): got = lax.all_to_all(values, axes, split_axis=0, concat_axis=0, tiled=True)  32.7 us
    pallas_call x6, Pallas kernels, run(): pl.pallas_call(kernel, in_specs=in_specs, out_specs=list(out_specs), out_...  31.8 us
    all_to_all x1, starting transfers between devices, exchange(): got = lax.all_to_all(values, axes, split_axis=0, concat_axis=0, tiled=True)  7.43 us
    unnamed x36, local copies, waits for them, and re-layouts  4.15 us
    all_to_all x1, waiting for transfers between devices, exchange(): got = lax.all_to_all(values, axes, split_axis=0, concat_axis=0, tiled=True)  3.45 us
  transfers between devices with their start and end apart: 1, of which 1 were waited for; matrix products, arithmetic and copies ran while one was open for 0% of the time, Pallas kernels for 3%

profile of v5, /device:TPU:0, one launch (start us, length us, event | category | flops | bytes accessed | tf_op | source)
XLA Modules:
  0.0 80.5 jit_solution(3365947206764663632)
XLA Ops:
  0.0 0.0 copy-start.15
  0.0 0.0 copy-start.16
  0.0 7.1 %first.1 = (bf16[1024,512]{1,0:T(8,128)(2,1)}, bf16[1024,512]{1,0:T(8,128)(2,1)}, bf16[1024,128]{1,0:T(8,128)(2,1)}, bf16[512,512]{1,0:T(8,128)(2,1)}, bf16[512,...) custom-call(bf16[2048,512]{1,0:T(8,128)(2,1)} %x_hbm.1, s32[32,64]{1,0:T(8,128)} %bitcast.19, ...), custom_call_target="tpu_custom_call" | custom-call | flops 1000000000 | bytes 8000000 | tf_op jit(solution)/shard_map/first/pallas_call | solution.py:523
  7.1 7.4 %all-to-all-start = ((bf16[32,32,128]{2,1,0:T(8,128)(2,1)}), bf16[32,32,128]{2,1,0:T(8,128)(2,1)}, u32[]{:S(2)}, u32[]{:S(2)}) async-start(bf16[32,32,128]{2,1,0:T(8,128)(2,1)} %bitcast.22), calls=%async_computation | async-start | bytes 524288 | tf_op jit(solution)/shard_map/all_to_all | solution.py:584
  15.2 0.0 copy-done.15
  15.2 0.0 copy-done.16
  15.3 0.0 copy-start.13
  15.3 1.6 %copy-done.13 = bf16[64,32,512]{2,1,0:T(8,128)(2,1)S(1)} copy-done((bf16[64,32,512]{2,1,0:T(8,128)(2,1)S(1)}, bf16[64,32,512]{2,1,0:T(8,128)(2,1)}, u32[]{:S(2)}) %copy-start.13) | copy-done | bytes 2097176
  16.9 0.0 copy-start.14
  16.9 0.9 %copy-done.14 = bf16[2,1024,64]{1,2,0:T(8,128)(2,1)S(1)} copy-done((bf16[2,1024,64]{1,2,0:T(8,128)(2,1)S(1)}, bf16[2,1024,64]{1,2,0:T(8,128)(2,1)}, u32[]{:S(2)}) %copy-start.14) | copy-done | bytes 262168
  17.8 0.0 copy-start.17
  17.8 0.7 copy-done.17
  18.5 2.4 %prepare.1 = (bf16[9,512,256]{2,1,0:T(8,128)(2,1)S(1)}, s32[9,256,128]{2,1,0:T(8,128)S(1)}, s32[5,256,128]{2,1,0:T(8,128)S(1)}) custom-call(s32[1]{0:T(128)S(6)} %copy.15.counts_ref, s32[1,2048]{1,0:T(1,128)S(1)} %copy-done.15, s32[1,2048]{1,0:T(1,128)S(1)} %copy-done.16, s32[1,1024]{1,0:T(1,128)S(1)} %copy-done.17, bf16[64,32,512]{2,1,0:T(8,128)(2,1)S(1)} %copy-done.13, ...), custom_call_target="tpu_custom_call" | custom-call | flops 4000000000 | bytes 8000000 | tf_op jit(solution)/shard_map/prepare/pallas_call | solution.py:523
  20.9 0.0 copy-start.2
  20.9 0.9 %copy-done.2 = s32[5,256,128]{2,1,0:T(8,128)} copy-done((s32[5,256,128]{2,1,0:T(8,128)}, s32[5,256,128]{2,1,0:T(8,128)S(1)}, u32[]{:S(2)}) %copy-start.2) | copy-done | bytes 655384
  21.8 3.5 %all-to-all-done = bf16[32,32,128]{2,1,0:T(8,128)(2,1)} async-done(((bf16[32,32,128]{2,1,0:T(8,128)(2,1)}), bf16[32,32,128]{2,1,0:T(8,128)(2,1)}, u32[]{:S(2)}, u32[]{:S(2)}) %all-to-all-start) | async-done | bytes 262176 | tf_op jit(solution)/shard_map/all_to_all | solution.py:584
  25.2 0.0 copy-start.3
  25.2 0.0 copy-start.5
  25.2 0.0 copy-start.6
  25.2 0.0 copy-start.7
  25.2 0.0 copy-start.8
  25.2 0.0 copy-start.9
  25.2 0.0 copy-start.10
  25.3 0.0 copy-start.11
  25.3 0.0 copy-start.12
  25.3 5.0 %owner.2 = bf16[256,256]{1,0:T(8,128)(2,1)S(1)} custom-call(bf16[1024,128]{1,0:T(8,128)(2,1)} %bitcast.3.arrived_ref, s32[9,256,128]{2,1,0:T(8,128)S(1)} %get-tuple-element.18.source_ref, bf16[9,512,256]{2,1,0:T(8,128)(2,1)S(1)} %get-tuple-element.19.basis_ref), custom_call_target="tpu_custom_call" | custom-call | flops 1000000000 | bytes 8000000 | tf_op jit(solution)/shard_map/owner/pallas_call | solution.py:523
  30.3 9.9 %all_to_all.20 = bf16[32,8,256]{2,1,0:T(8,128)(2,1)S(1)} all-to-all(bf16[32,8,256]{2,1,0:T(8,128)(2,1)S(1)} %bitcast.17), channel_id=1, replica_groups=mesh['bond'=4,'atom'=8] {'bond','atom'}, dimensions={0} | all-to-all | bytes 262144 | tf_op jit(solution)/shard_map/all_to_all | solution.py:584
  40.2 0.0 copy-done.3
  40.2 0.0 copy-done.5
  40.2 0.0 copy-done.6
  40.2 0.0 copy-done.7
  40.2 0.0 copy-done.8
  40.2 0.0 copy-done.9
  40.2 0.0 copy-done.10
  40.2 0.0 copy-done.11
  40.2 0.0 copy-done.12
  40.2 8.3 %middle.1 = (bf16[2048,512]{1,0:T(8,128)(2,1)}, bf16[1024,128]{1,0:T(8,128)(2,1)S(1)}) custom-call(bf16[256,256]{1,0:T(8,128)(2,1)S(1)} %bitcast.15, s32[5,256,128]{2,1,0:T(8,128)S(1)} %copy-done.3, bf16[1024,512]{1,0:T(8,128)(2,1)S(1)} %copy-done.5, bf16[1024,512]{1,0:T(8,128)(2,1)} %get-tuple-element.22.x_high_hbm, bf16[2,64,512]{2,1,0:T(8,128)(2,1)S(1)} %copy-done.6, ...), custom_call_target="tpu_custom_call" | custom-call | flops 1000000000 | bytes 8000000 | tf_op jit(solution)/shard_map/middle/pallas_call | solution.py:523
  48.6 12.9 %all_to_all.21 = bf16[32,32,128]{2,1,0:T(8,128)(2,1)S(1)} all-to-all(bf16[32,32,128]{2,1,0:T(8,128)(2,1)S(1)} %bitcast.18), channel_id=1, replica_groups=mesh['bond'=4,'atom'=8] {'bond','atom'}, dimensions={0} | all-to-all | bytes 524288 | tf_op jit(solution)/shard_map/all_to_all | solution.py:584
  61.5 0.0 copy-start
  61.5 0.0 copy-start.1
  61.5 0.0 copy-start.4
  61.5 3.9 %owner.3 = bf16[256,256]{1,0:T(8,128)(2,1)S(1)} custom-call(bf16[1024,128]{1,0:T(8,128)(2,1)S(1)} %bitcast.11, s32[9,256,128]{2,1,0:T(8,128)S(1)} %get-tuple-element.18.source_ref, bf16[9,512,256]{2,1,0:T(8,128)(2,1)S(1)} %get-tuple-element.19.basis_ref), custom_call_target="tpu_custom_call" | custom-call | flops 1000000000 | bytes 8000000 | tf_op jit(solution)/shard_map/owner/pallas_call | solution.py:523
  65.4 9.9 %all_to_all.22 = bf16[32,8,256]{2,1,0:T(8,128)(2,1)S(1)} all-to-all(bf16[32,8,256]{2,1,0:T(8,128)(2,1)S(1)} %bitcast.16), channel_id=1, replica_groups=mesh['bond'=4,'atom'=8] {'bond','atom'}, dimensions={0} | all-to-all | bytes 262144 | tf_op jit(solution)/shard_map/all_to_all | solution.py:584
  75.3 0.0 copy-done
  75.3 0.0 copy-done.1
  75.4 0.0 copy-done.4
  75.4 5.0 %last.1 = bf16[2048,512]{1,0:T(8,128)(2,1)} custom-call(bf16[256,256]{1,0:T(8,128)(2,1)S(1)} %bitcast.12, s32[5,256,128]{2,1,0:T(8,128)S(1)} %copy-done.3, bf16[2048,512]{1,0:T(8,128)(2,1)S(1)} %copy-done.4, bf16[2,64,512]{2,1,0:T(8,128)(2,1)S(1)} %copy-done.6, bf16[2,512,512]{2,1,0:T(8,128)(2,1)S(1)} %copy-done, bf16[2,512,512]{2,1,0:T(8,128)(2,1)S(1)} %copy-done.1), custom_call_target="tpu_custom_call" | custom-call | flops 1000000000 | bytes 8000000 | tf_op jit(solution)/shard_map/last/pallas_call | solution.py:523
Async XLA Ops:
  0.0 15.2 %copy-start.15 = (s32[1,2048]{1,0:T(1,128)S(1)}, s32[1,2048]{1,0:T(1,128)}, u32[]{:S(2)}) copy-start(s32[1,2048]{1,0:T(1,128)} %source_ref.1) | copy-start | bytes 24580
  0.0 15.2 %copy-start.16 = (s32[1,2048]{1,0:T(1,128)S(1)}, s32[1,2048]{1,0:T(1,128)}, u32[]{:S(2)}) copy-start(s32[1,2048]{1,0:T(1,128)} %target_ref.1) | copy-start | bytes 24580
  7.1 18.1 %all-to-all-start = ((bf16[32,32,128]{2,1,0:T(8,128)(2,1)}), bf16[32,32,128]{2,1,0:T(8,128)(2,1)}, u32[]{:S(2)}, u32[]{:S(2)}) async-start(bf16[32,32,128]{2,1,0:T(8,128)(2,1)} %bitcast.22), calls=%async_computation | async-start | bytes 524288 | tf_op jit(solution)/shard_map/all_to_all | solution.py:584
  15.3 1.6 %copy-start.13 = (bf16[64,32,512]{2,1,0:T(8,128)(2,1)S(1)}, bf16[64,32,512]{2,1,0:T(8,128)(2,1)}, u32[]{:S(2)}) copy-start(bf16[64,32,512]{2,1,0:T(8,128)(2,1)} %basis_hbm.1) | copy-start | bytes 6291460
  16.9 0.9 %copy-start.14 = (bf16[2,1024,64]{1,2,0:T(8,128)(2,1)S(1)}, bf16[2,1024,64]{1,2,0:T(8,128)(2,1)}, u32[]{:S(2)}) copy-start(bf16[2,1024,64]{1,2,0:T(8,128)(2,1)} %param.24) | copy-start | bytes 786436
  17.8 0.7 copy-start.17
  20.9 0.9 %copy-start.2 = (s32[5,256,128]{2,1,0:T(8,128)}, s32[5,256,128]{2,1,0:T(8,128)S(1)}, u32[]{:S(2)}) copy-start(s32[5,256,128]{2,1,0:T(8,128)S(1)} %get-tuple-element.20.return_low_ref) | copy-start | bytes 1966084
  25.2 15.0 %copy-start.3 = (s32[5,256,128]{2,1,0:T(8,128)S(1)}, s32[5,256,128]{2,1,0:T(8,128)}, u32[]{:S(2)}) copy-start(s32[5,256,128]{2,1,0:T(8,128)} %copy-done.2) | copy-start | bytes 1966084
  25.2 15.0 %copy-start.5 = (bf16[1024,512]{1,0:T(8,128)(2,1)S(1)}, bf16[1024,512]{1,0:T(8,128)(2,1)}, u32[]{:S(2)}) copy-start(bf16[1024,512]{1,0:T(8,128)(2,1)} %get-tuple-element.21.x_low_ref) | copy-start | bytes 3145732
  25.2 15.0 %copy-start.6 = (bf16[2,64,512]{2,1,0:T(8,128)(2,1)S(1)}, bf16[2,64,512]{2,1,0:T(8,128)(2,1)}, u32[]{:S(2)}) copy-start(bf16[2,64,512]{2,1,0:T(8,128)(2,1)} %up_ref.3) | copy-start | bytes 393220
  25.2 15.0 %copy-start.7 = (bf16[512,512]{1,0:T(8,128)(2,1)S(1)}, bf16[512,512]{1,0:T(8,128)(2,1)}, u32[]{:S(2)}) copy-start(bf16[512,512]{1,0:T(8,128)(2,1)} %get-tuple-element.23.post_inner_ref) | copy-start | bytes 1572868
  25.2 15.0 %copy-start.8 = (bf16[512,512]{1,0:T(8,128)(2,1)S(1)}, bf16[512,512]{1,0:T(8,128)(2,1)}, u32[]{:S(2)}) copy-start(bf16[512,512]{1,0:T(8,128)(2,1)} %get-tuple-element.24.post_outer_ref) | copy-start | bytes 1572868
  25.2 15.0 %copy-start.9 = (bf16[512,512]{1,0:T(8,128)(2,1)S(1)}, bf16[512,512]{1,0:T(8,128)(2,1)}, u32[]{:S(2)}) copy-start(bf16[512,512]{1,0:T(8,128)(2,1)} %get-tuple-element.25.inner_ref) | copy-start | bytes 1572868
  25.2 15.0 %copy-start.10 = (bf16[512,512]{1,0:T(8,128)(2,1)S(1)}, bf16[512,512]{1,0:T(8,128)(2,1)}, u32[]{:S(2)}) copy-start(bf16[512,512]{1,0:T(8,128)(2,1)} %get-tuple-element.26.outer_ref) | copy-start | bytes 1572868
  25.3 15.0 %copy-start.11 = (bf16[2,512,64]{1,2,0:T(8,128)(2,1)S(1)}, bf16[2,512,64]{1,2,0:T(8,128)(2,1)}, u32[]{:S(2)}) copy-start(bf16[2,512,64]{1,2,0:T(8,128)(2,1)} %param.23) | copy-start | bytes 393220
  25.3 15.0 %copy-start.12 = (s32[1,32,64]{2,1,0:T(8,128)S(1)}, s32[1,32,64]{2,1,0:T(8,128)}, u32[]{:S(2)}) copy-start(s32[1,32,64]{2,1,0:T(8,128)} %param.16) | copy-start | bytes 24580
  61.5 13.9 %copy-start = (bf16[2,512,512]{2,1,0:T(8,128)(2,1)S(1)}, bf16[2,512,512]{2,1,0:T(8,128)(2,1)}, u32[]{:S(2)}) copy-start(bf16[2,512,512]{2,1,0:T(8,128)(2,1)} %post_inner_ref.1) | copy-start | bytes 3145732
  61.5 13.9 %copy-start.1 = (bf16[2,512,512]{2,1,0:T(8,128)(2,1)S(1)}, bf16[2,512,512]{2,1,0:T(8,128)(2,1)}, u32[]{:S(2)}) copy-start(bf16[2,512,512]{2,1,0:T(8,128)(2,1)} %post_outer_ref.1) | copy-start | bytes 3145732
  61.5 13.9 %copy-start.4 = (bf16[2048,512]{1,0:T(8,128)(2,1)S(1)}, bf16[2048,512]{1,0:T(8,128)(2,1)}, u32[]{:S(2)}) copy-start(bf16[2048,512]{1,0:T(8,128)(2,1)} %get-tuple-element.28.x_ref) | copy-start | bytes 6291460
